TPU v7x, 256 devices: a whole 4x4x8 slice. The times are simulated.
256 devices in a mesh: group: 16 (over x, y_hi, core), fsdp: 16 (over z, y_lo).
Axes of the slice: x: 4, y: 4 (y_hi: 2, y_lo: 2; y = y_hi * 2 + y_lo), z: 8, core: 2. Of those that a mesh axis runs over, the one named last changes fastest.
Arguments:
- features: bfloat16 [16, 4096, 5120], P('group', 'fsdp'), may hold values from -6 to 6
- value_cotangent: bfloat16 [16, 4096, 1024], P('group', 'fsdp'), may hold values from -6 to 6
- params: float32 [16, 5120, 1024], P('group', 'fsdp'), may hold values from -0.078125 to 0.078125
- momentum: float32 [16, 5120, 1024], P('group', 'fsdp'), may hold values from -0.12 to 0.12
- step_index: int32 [1], replicated, may hold values from 0 to 999
Outputs:
- input_grad: bfloat16 [16, 4096, 5120], P('group', 'fsdp')
- new_params: float32 [16, 5120, 1024], P('group', 'fsdp')
- new_momentum: float32 [16, 5120, 1024], P('group', 'fsdp')
All inputs are finite; a program needn't handle non-finite values.
Results may differ from a plain program's by a relative error of at most 0.0049.
Values may be sent and summed in bfloat16 or wider, within the bound.
No kernel may reach another device: no remote copies, remote signals or barrier semaphores. Data moves between devices by JAX's collectives and lax.ppermute only.
A program may use at most 128 MiB of HBM per device.

v0:
```python
from functools import partial

import jax
import jax.numpy as jnp
from jax import lax
from jax.experimental import pallas as pl
from jax.experimental.pallas import tpu as pltpu
from jax.sharding import PartitionSpec as P

BF16 = jnp.bfloat16
F32 = jnp.float32
RING = 8
PAIR = 2
FAR = RING // 2
KERNEL_BYTES = 8 * 1024 * 1024
ANY = pl.BlockSpec(memory_space=pl.ANY)
VMEM = pl.BlockSpec(memory_space=pltpu.VMEM)
TOKEN = jax.ShapeDtypeStruct((8, 128), F32)
PARAMS = pltpu.CompilerParams(vmem_limit_bytes=KERNEL_BYTES)

ROUNDS = tuple(
    zip(
        ("wb1", "wa1", "wb2", "wa2", "wb3", "wa3", "wb4", "sa1", "sb1", "sa2", "sb2", "sa3", "sb3", "sa4"),
        ("wa1", "wb1", "wa2", "wb2", "wa3", "wb3", "wa4", "sb1", "sa1", "sb2", "sa2", "sb3", "sa3", "sb4"),
        strict=True,
    )
)
G1, G2 = 6, 9
PRODUCTS = (((1, -1, 2, -2), 5), ((3, -3, 0, 4), 8))
JOINS = (11, 12)
SETTLE = 10
REACH = {"wa": (3, 4), "wb": (4, 3), "sa": (4, 3), "sb": (3, 4)}
SIGNS = (1, -1)
SIDES = "ab"
FIRST = (FAR, FAR - 1, 1 - FAR)
SECOND = (2, -2, 1, -1, 0)


def along_z(part, by):
    length = RING * PAIR
    return lax.ppermute(part, "fsdp", [(i, (i + PAIR * by) % length) for i in range(length)])


def across_pair(part):
    return lax.ppermute(part, "fsdp", [(i, i ^ 1) for i in range(RING * PAIR)])


def along_group(part, by):
    length = lax.axis_size("group")
    return lax.ppermute(part, "group", [(i, (i + by) % length) for i in range(length)])


def cost(flops, touched):
    return pl.CostEstimate(flops=flops, bytes_accessed=touched, transcendentals=0)


def here():
    index = lax.axis_index("fsdp")
    ahead = (index // PAIR + jnp.arange(RING, dtype=jnp.int32)) % RING
    return jnp.concatenate([(index % PAIR)[None], ahead]).astype(jnp.int32)


def block_at(where_ref, i, distances):
    at = distances[-1] % RING
    for j, distance in enumerate(distances[:-1]):
        at = jnp.where(i == j, distance % RING, at)
    return where_ref[1 + at]


def in_vmem(kernel, operands, after, outs, flops=0, aliases=None):
    inputs = len(operands)

    def body(*refs):
        kernel(*refs[:inputs], *refs[inputs + len(after) : -1])
        refs[-1][...] = jnp.zeros(TOKEN.shape, TOKEN.dtype)

    return pl.pallas_call(
        body,
        in_specs=[VMEM] * (inputs + len(after)),
        out_specs=[VMEM] * (len(outs) + 1),
        out_shape=[*(jax.ShapeDtypeStruct(shape, kind) for shape, kind in outs), TOKEN],
        input_output_aliases=aliases or {},
        compiler_params=PARAMS,
        cost_estimate=cost(flops, 0),
    )(*operands, *after)


def by_tiles(rows, body, tile=32):
    @pl.loop(0, rows // tile)
    def _(i):
        body(pl.ds(pl.multiple_of(i * tile, tile), tile))


def serve(passed, sums, after):
    count = len(passed)

    def kernel(*refs):
        ins, outs = refs[: count + 2 * len(sums)], refs[count + 2 * len(sums) :]
        for k in range(count):

            def copy(tile, k=k):
                outs[k][tile, :] = ins[k][tile, :]

            by_tiles(passed[k].shape[0], copy)
        for k, (_, arrived) in enumerate(sums):
            term_ref, arrived_ref = ins[count + 2 * k : count + 2 * k + 2]

            def add(tile, k=k, term_ref=term_ref, arrived_ref=arrived_ref):
                total = term_ref[tile, :] + arrived_ref[tile, :].astype(F32)
                outs[count + k][tile, :] = total.astype(BF16)

            by_tiles(arrived.shape[0], add)

    operands = [*passed, *(part for pair in sums for part in pair)]
    outs = [(a.shape, a.dtype) for a in passed] + [(a.shape, BF16) for _, a in sums]
    *made, token = in_vmem(kernel, operands, after, outs, 0, {k: k for k in range(count)})
    return made[:count], made[count:], token


def split_kernel(where_ref, features_ref, *refs):
    mine_ref, theirs_ref, token_ref = refs[-3:]
    half = mine_ref.shape[0]
    turned = features_ref[...].T
    even = where_ref[0] == 0
    mine_ref[...] = jnp.where(even, turned[:half], turned[half:])
    theirs_ref[...] = jnp.where(even, turned[half:], turned[:half])
    token_ref[...] = jnp.zeros(TOKEN.shape, TOKEN.dtype)


def split_features(features, where, distances, after):
    tokens, width = features.shape
    block = width // RING
    half = block // PAIR
    count = len(distances)
    out = jax.ShapeDtypeStruct((count * half, tokens), features.dtype)
    return pl.pallas_call(
        split_kernel,
        grid_spec=pltpu.PrefetchScalarGridSpec(
            num_scalar_prefetch=1,
            grid=(count,),
            in_specs=[
                pl.BlockSpec(
                    (tokens, block), lambda i, where_ref: (0, block_at(where_ref, i, distances))
                ),
                *[VMEM] * len(after),
            ],
            out_specs=[pl.BlockSpec((half, tokens), lambda i, where_ref: (i, 0))] * 2 + [VMEM],
        ),
        out_shape=[out, out, TOKEN],
        compiler_params=PARAMS,
        cost_estimate=cost(0, 4 * count * tokens * block),
    )(where, features, *after)


def terms(mine, theirs, cotans, kinds, after):
    own, other = cotans
    tokens, width = own.shape
    count = len(kinds)
    rows = mine.shape[0] // count
    half = width // 2

    def kernel(mine_ref, theirs_ref, own_ref, other_ref, *out_refs):
        for i in range(count):
            block = slice(i * rows, (i + 1) * rows)
            for j in range(2):
                cut = slice(j * half, (j + 1) * half)
                out_ref = out_refs[2 * i + j]
                out_ref[...] = (
                    jnp.dot(mine_ref[block, :], own_ref[:, cut], preferred_element_type=F32)
                    + jnp.dot(theirs_ref[block, :], other_ref[:, cut], preferred_element_type=F32)
                ).astype(out_ref.dtype)

    outs = [((rows, half), kind) for pair in kinds for kind in pair]
    *made, token = in_vmem(
        kernel, [mine, theirs, own, other], after, outs, 4 * count * tokens * rows * width
    )
    return [tuple(made[2 * i : 2 * i + 2]) for i in range(count)], token


def products(cotans, weights, after):
    own, other = cotans
    tokens, depth = own.shape
    half = depth // 2
    count = len(weights)
    rows = weights[0][0].shape[0]

    def kernel(own_ref, other_ref, *refs):
        for i in range(count):
            for cotan_ref, out_ref in ((other_ref, refs[-1]), (own_ref, refs[-2])):
                total = sum(
                    lax.dot_general(
                        cotan_ref[:, j * half : (j + 1) * half],
                        refs[2 * i + j][...],
                        (((1,), (1,)), ((), ())),
                        preferred_element_type=F32,
                    )
                    for j in range(2)
                )
                out_ref[:, i * rows : (i + 1) * rows] = total.astype(BF16)

    return in_vmem(
        kernel,
        [own, other, *(part for block in weights for part in block)],
        after,
        [((tokens, count * rows), BF16)] * 2,
        4 * count * tokens * depth * rows,
    )


def join(own, arrived, where, distances, into, after):
    tokens, width = own.shape
    count = len(distances)
    rows = width // count

    def kernel(where_ref, own_ref, arrived_ref, *refs):
        out_ref, token_ref = refs[-2:]
        even = where_ref[0] == 0
        token_ref[...] = jnp.zeros(TOKEN.shape, TOKEN.dtype)
        for i in range(count):

            @pl.when(pl.program_id(0) == i)
            def _(i=i):
                cut = slice(i * rows, (i + 1) * rows)
                mine, theirs = own_ref[:, cut], arrived_ref[:, cut]
                out_ref[:, :rows] = jnp.where(even, mine, theirs)
                out_ref[:, rows:] = jnp.where(even, theirs, mine)

    whole = pl.BlockSpec((tokens, width), lambda i, where_ref: (0, 0))
    operands, in_specs, aliases = [own, arrived, *after], [whole, whole, *[VMEM] * len(after)], {}
    if into is not None:
        operands.append(into)
        in_specs.append(ANY)
        aliases = {len(operands): 0}
    return pl.pallas_call(
        kernel,
        grid_spec=pltpu.PrefetchScalarGridSpec(
            num_scalar_prefetch=1,
            grid=(count,),
            in_specs=in_specs,
            out_specs=[
                pl.BlockSpec(
                    (tokens, PAIR * rows),
                    lambda i, where_ref: (0, block_at(where_ref, i, distances)),
                ),
                VMEM,
            ],
        ),
        out_shape=[jax.ShapeDtypeStruct((tokens, RING * PAIR * rows), BF16), TOKEN],
        input_output_aliases=aliases,
        compiler_params=PARAMS,
        cost_estimate=cost(0, 8 * count * tokens * rows),
    )(where, *operands)


def shorten(weights):
    rows, width = weights.shape
    half = width // 2

    def kernel(weights_ref, left_ref, right_ref):
        def short(tile):
            left_ref[tile, :] = weights_ref[tile, :half].astype(BF16)
            right_ref[tile, :] = weights_ref[tile, half:].astype(BF16)

        by_tiles(rows, short)

    return in_vmem(kernel, [weights], (), [((rows, half), BF16)] * 2)[:2]


def settle(own, moment, count, after):
    rows, half = own[0].shape

    def kernel(left_ref, right_ref, moment_ref, out_ref):
        def add(tile):
            out_ref[tile, :half] = 0.9 * moment_ref[tile, :half] + left_ref[tile, :] / count
            out_ref[tile, half:] = 0.9 * moment_ref[tile, half:] + right_ref[tile, :] / count

        by_tiles(rows, add)

    return in_vmem(kernel, [*own, moment], after, [(moment.shape, F32)])


def fold(settled, arrived, weights, count, after):
    rows, width = weights.shape
    half = width // 2

    def kernel(settled_ref, left_ref, right_ref, weights_ref, momentum_ref, stepped_ref):
        for j, arrived_ref in enumerate((left_ref, right_ref)):
            cut = slice(j * half, (j + 1) * half)

            def add(tile, cut=cut, arrived_ref=arrived_ref):
                momentum = settled_ref[tile, cut] + arrived_ref[tile, :].astype(F32) / count
                momentum_ref[tile, cut] = momentum
                stepped_ref[tile, cut] = weights_ref[tile, cut] - 0.5 * momentum

            by_tiles(rows, add)

    outs = [((rows, width), F32)] * 2
    return in_vmem(kernel, [settled, *arrived, weights], after, outs)


def stepped_short(stepped, arrived, count):
    rows, width = stepped.shape
    half = width // 2

    def kernel(stepped_ref, left_ref, right_ref, out_ref):
        for j, arrived_ref in enumerate((left_ref, right_ref)):
            cut = slice(j * half, (j + 1) * half)

            def add(tile, cut=cut, arrived_ref=arrived_ref):
                last = arrived_ref[tile, :].astype(F32) / count
                out_ref[tile, cut] = (stepped_ref[tile, cut] - 0.5 * last).astype(BF16)

            by_tiles(rows, add)

    return in_vmem(kernel, [stepped, *arrived], (), [((rows, width), BF16)])[0]


def mix(stepped, arrived):
    rows, width = stepped.shape
    tile = rows // 4

    def kernel(stepped_ref, arrived_ref, out_ref):
        def mean(rows):
            out_ref[rows, :] = 0.5 * (stepped_ref[rows, :] + arrived_ref[rows, :].astype(F32))

        by_tiles(tile, mean, 16)

    block = pl.BlockSpec((tile, width), lambda i: (i, 0))
    return pl.pallas_call(
        kernel,
        grid=(4,),
        in_specs=[block, block],
        out_specs=block,
        out_shape=jax.ShapeDtypeStruct(stepped.shape, F32),
        compiler_params=PARAMS,
        cost_estimate=cost(0, 0),
    )(stepped, arrived)


def finish(short, settled, arrived, weights, by, count):
    other = along_group(short, by)
    momentum, stepped, _ = fold(settled, arrived, weights, count, ())
    return mix(stepped, other), momentum


def step(features, cotan, weights, moment, level, hops):
    where = here()
    tokens, width = cotan.shape
    count = tokens * RING * PAIR
    own = dict(zip(SIDES, shorten(weights), strict=True))
    cotans = (cotan, across_pair(cotan))

    term, held, landed, flying = {}, {0: (own["a"], own["b"])}, {}, {}
    more = new_params = input_grad = None
    pieces = []

    def payload(side_way, name):
        chain, number = name[:2], int(name[2])
        if number > 1:
            arrived = landed.get((side_way, chain + str(number - 1)))
            if chain[0] == "w":
                return arrived, None
            left = REACH[chain][side_way] - number + 1
            return arrived, term[SIGNS[side_way] * left][SIDES.index(chain[1])]
        if chain[0] == "w":
            return own[chain[1]], None
        far = REACH[chain][side_way]
        return term[far if far == FAR else SIGNS[side_way] * far][SIDES.index(chain[1])], None

    mine, theirs, token = split_features(features, where, FIRST, ())
    blocks = (mine, across_pair(theirs))
    after = [token]
    for number in range(len(ROUNDS)):
        if number >= 2:
            names = [(way, ROUNDS[number - 2][way]) for way in range(2)]
            arrays = [flying[name] for name in names]
            landed.update(zip(names, arrays, strict=True))
            sums, kept = [], {}
            for way in range(2):
                array, addend = payload(way, ROUNDS[number][way])
                if addend is None:
                    kept[way] = array
                else:
                    sums.append((addend, array))
            passed, keys = [], []
            for key, array in [*zip(names, arrays, strict=True), *kept.items()]:
                if not any(array is one for one in passed) and not any(array is pair[1] for pair in sums):
                    passed.append(array)
                    keys.append(key)
            extra = []
            if number == 3:
                extra = [cotans[1]]
            if number == G1:
                extra = [blocks[1]]
            if number == G2:
                extra = [more[1]]
            handed, summed, token = serve([*passed, *extra], sums, after)
            if number == 3:
                cotans = (cotan, handed[-1])
            if number == G1:
                blocks = (mine, handed[-1])
            if number == G2:
                more = (more[0], handed[-1])
            after = [token]
            again = {id(a): b for a, b in zip(passed, handed)}
            for name in names:
                landed[name] = again.get(id(landed[name]))
            sends = []
            for way in range(2):
                sends.append(again[id(kept[way])] if way in kept else summed.pop(0))
            for way in range(2):
                name = ROUNDS[number][way]
                if way in kept and name[0] == "w" and name[2] != "1":
                    landed[way, name[:2] + str(int(name[2]) - 1)] = sends[way]
        else:
            sends = [payload(way, ROUNDS[number][way])[0] for way in range(2)]
        for way in range(2):
            flying[way, ROUNDS[number][way]] = along_z(sends[way], SIGNS[way])

        for some, at in PRODUCTS:
            if at != number:
                continue
            for d in some:
                key = str(abs(d))
                if d == FAR:
                    held[d] = (landed[1, "wa" + key], landed[0, "wb" + key])
                elif d:
                    way = 1 if d > 0 else 0
                    held[d] = (landed[way, "wa" + key], landed[way, "wb" + key])
            ours, others, token = products(cotans, [held[d] for d in some], after)
            after = [token]
            pieces.append((ours, across_pair(others), some))
        if number == 2:
            rest, theirs, token = split_features(features, where, SECOND, after)
            more = (rest, across_pair(theirs))
            after = [token]
        if number == G1:
            kinds = ((BF16, BF16), (F32, BF16), (BF16, F32))
            made, token = terms(*blocks, cotans, kinds, after)
            term.update(zip(FIRST, made, strict=True))
            after = [token]
        if number == G2:
            made, token = terms(*more, cotans, ((F32, F32),) * 5, after)
            term.update(zip(SECOND, made, strict=True))
            after = [token]
        if number in JOINS:
            ours, others, some = pieces.pop(0)
            input_grad, token = join(ours, others, where, some, input_grad, after)
            after = [token]
        if number == SETTLE:
            settled, token = settle(term[0], moment, count, after)
            after = [token]

    early = [flying[1, "sa3"], flying[0, "sb3"]]
    settled, stepped, _ = fold(settled, early, weights, count, after)
    arrived = [flying[0, "sa4"], flying[1, "sb4"]]
    short = stepped_short(stepped, arrived, count)
    branches = [partial(finish, by=by, count=count) for by in hops]
    new_params, momentum = lax.switch(level, branches, short, settled, arrived, weights)
    return input_grad, new_params, momentum


def per_device(features, value_cotangent, params, momentum, step_index):
    levels = lax.axis_size("group").bit_length() - 1
    outs = step(
        features[0],
        value_cotangent[0],
        params[0],
        momentum[0],
        step_index[0] % levels,
        [2**i for i in range(levels)],
    )
    return tuple(out[None] for out in outs)


def solution(mesh):
    in_specs = (
        P("group", "fsdp", None),
        P("group", "fsdp", None),
        P("group", "fsdp", None),
        P("group", "fsdp", None),
        P(),
    )
    out_specs = (P("group", "fsdp", None), P("group", "fsdp", None), P("group", "fsdp", None))
    return jax.shard_map(
        per_device, mesh=mesh, in_specs=in_specs, out_specs=out_specs, check_vma=False
    )
```

profile of v0, /device:TPU:2, one launch (start us, length us, event | category | flops | bytes accessed | tf_op | source)
XLA Modules:
  0.0 128.3 jit_solution(7078275131530020708)
XLA Ops:
  2.3 2.0 %shard_map.76 = (bf16[320,512]{1,0:T(8,128)(2,1)S(1)}, bf16[320,512]{1,0:T(8,128)(2,1)S(1)}, f32[8,128]{1,0:T(8,128)}) custom-call(f32[320,1024]{1,0:T(8,128)} %bitcast.23), custom_call_target="tpu_custom_call" | custom-call | tf_op jit(solution)/shard_map/pallas_call | solution.py:77
  6.2 3.9 %collective-permute-start.8 = (bf16[320,512]{1,0:T(8,128)(2,1)S(1)}, bf16[320,512]{1,0:T(8,128)(2,1)S(1)}, u32[]{:S(2)}, u32[]{:S(2)}) collective-permute-start(bf16[320,512]{1,0:T(8,128)(2,1)S(1)} %get-tuple-element.158.refs_6_), channel_id=1, source_target_pairs={{0,14},{1,15},{2,0},{3,1},{4,2},{5,3},{6,4},{7,5},{8,6},{9,7},{10,... | collective-permute-start | bytes 983048 | tf_op jit(solution)/shard_map/ppermute | solution.py:41
  10.1 3.2 %collective-permute-start.5 = (bf16[320,512]{1,0:T(8,128)(2,1)S(1)}, bf16[320,512]{1,0:T(8,128)(2,1)S(1)}, u32[]{:S(2)}, u32[]{:S(2)}) collective-permute-start(bf16[320,512]{1,0:T(8,128)(2,1)S(1)} %get-tuple-element.159.refs_7_), channel_id=1, source_target_pairs={{0,14},{1,15},{2,0},{3,1},{4,2},{5,3},{6,4},{7,5},{8,6},{9,7},{10,... | collective-permute-start | bytes 983048 | tf_op jit(solution)/shard_map/ppermute | solution.py:41
  16.4 2.3 %collective-permute-done.7.refs_0_ = bf16[320,512]{1,0:T(8,128)(2,1)S(1)} collective-permute-done((bf16[320,512]{1,0:T(8,128)(2,1)S(1)}, bf16[320,512]{1,0:T(8,128)(2,1)S(1)}, u32[]{:S(2)}, u32[]{:S(2)}) %collective-permute-start.7) | collective-permute-done | bytes 327712 | tf_op jit(solution)/shard_map/ppermute | solution.py:41
  19.0 3.3 %collective-permute-start.10 = (bf16[320,512]{1,0:T(8,128)(2,1)S(1)}, bf16[320,512]{1,0:T(8,128)(2,1)S(1)}, u32[]{:S(2)}, u32[]{:S(2)}) collective-permute-start(bf16[320,512]{1,0:T(8,128)(2,1)S(1)} %get-tuple-element.165.refs_2_), channel_id=1, source_target_pairs={{0,14},{1,15},{2,0},{3,1},{4,2},{5,3},{6,4},{7,5},{8,6},{9,7},{10,... | collective-permute-start | bytes 983048 | tf_op jit(solution)/shard_map/ppermute | solution.py:41
  22.3 3.5 %collective-permute-done.4.refs_0_ = bf16[320,512]{1,0:T(8,128)(2,1)S(1)} collective-permute-done((bf16[320,512]{1,0:T(8,128)(2,1)S(1)}, bf16[320,512]{1,0:T(8,128)(2,1)S(1)}, u32[]{:S(2)}, u32[]{:S(2)}) %collective-permute-start.4) | collective-permute-done | bytes 327712 | tf_op jit(solution)/shard_map/ppermute | solution.py:41
  28.1 3.2 %collective-permute-start.15 = (bf16[320,512]{1,0:T(8,128)(2,1)S(1)}, bf16[320,512]{1,0:T(8,128)(2,1)S(1)}, u32[]{:S(2)}, u32[]{:S(2)}) collective-permute-start(bf16[320,512]{1,0:T(8,128)(2,1)S(1)} %get-tuple-element.170.refs_3_), channel_id=1, source_target_pairs={{0,14},{1,15},{2,0},{3,1},{4,2},{5,3},{6,4},{7,5},{8,6},{9,7},{10,... | collective-permute-start | bytes 983048 | tf_op jit(solution)/shard_map/ppermute | solution.py:41
  33.1 3.2 %collective-permute-start.12 = (bf16[320,512]{1,0:T(8,128)(2,1)S(1)}, bf16[320,512]{1,0:T(8,128)(2,1)S(1)}, u32[]{:S(2)}, u32[]{:S(2)}) collective-permute-start(bf16[320,512]{1,0:T(8,128)(2,1)S(1)} %get-tuple-element.168.refs_6_), channel_id=1, source_target_pairs={{0,14},{1,15},{2,0},{3,1},{4,2},{5,3},{6,4},{7,5},{8,6},{9,7},{10,... | collective-permute-start | bytes 983048 | tf_op jit(solution)/shard_map/ppermute | solution.py:41
  36.3 3.6 %collective-permute-done.14.refs_0_ = bf16[320,512]{1,0:T(8,128)(2,1)S(1)} collective-permute-done((bf16[320,512]{1,0:T(8,128)(2,1)S(1)}, bf16[320,512]{1,0:T(8,128)(2,1)S(1)}, u32[]{:S(2)}, u32[]{:S(2)}) %collective-permute-start.14) | collective-permute-done | bytes 327712 | tf_op jit(solution)/shard_map/ppermute | solution.py:41
  41.8 3.2 %collective-permute-start.17 = (bf16[320,512]{1,0:T(8,128)(2,1)S(1)}, bf16[320,512]{1,0:T(8,128)(2,1)S(1)}, u32[]{:S(2)}, u32[]{:S(2)}) collective-permute-start(bf16[320,512]{1,0:T(8,128)(2,1)S(1)} %get-tuple-element.173.refs_7_), channel_id=1, source_target_pairs={{0,14},{1,15},{2,0},{3,1},{4,2},{5,3},{6,4},{7,5},{8,6},{9,7},{10,... | collective-permute-start | bytes 983048 | tf_op jit(solution)/shard_map/ppermute | solution.py:41
  45.0 2.4 %shard_map.83 = (bf16[256,1280]{1,0:T(8,128)(2,1)S(1)}, bf16[256,1280]{1,0:T(8,128)(2,1)S(1)}, f32[8,128]{1,0:T(8,128)S(1)}) custom-call(bf16[256,1024]{1,0:T(8,128)(2,1)S(1)} %bitcast.19, bf16[256,1024]{1,0:T(8,128)(2,1)S(1)} %get-tuple-element.163.refs_1_.refs_3_, bf16[320,512]{1,0:T(8,128)(2,1)S(1)} %get-tuple-element.165.refs_2_, ...), custom_call_target="tpu_custom_call" | custom-call | flops 1342177280 | tf_op jit(solution)/shard_map/pallas_call | solution.py:77
  47.9 3.2 %collective-permute-start.19 = (bf16[320,512]{1,0:T(8,128)(2,1)S(1)}, bf16[320,512]{1,0:T(8,128)(2,1)S(1)}, u32[]{:S(2)}, u32[]{:S(2)}) collective-permute-start(bf16[320,512]{1,0:T(8,128)(2,1)S(1)} %get-tuple-element.177.refs_2_), channel_id=1, source_target_pairs={{0,14},{1,15},{2,0},{3,1},{4,2},{5,3},{6,4},{7,5},{8,6},{9,7},{10,... | collective-permute-start | bytes 983048 | tf_op jit(solution)/shard_map/ppermute | solution.py:41
  54.4 3.3 %collective-permute-start.23 = (bf16[320,512]{1,0:T(8,128)(2,1)S(1)}, bf16[320,512]{1,0:T(8,128)(2,1)S(1)}, u32[]{:S(2)}, u32[]{:S(2)}) collective-permute-start(bf16[320,512]{1,0:T(8,128)(2,1)S(1)} %get-tuple-element.200), channel_id=1, source_target_pairs={{0,14},{1,15},{2,0},{3,1},{4,2},{5,3},{6,4},{7,5},{8,6},{9,7},{10,... | collective-permute-start | bytes 983048 | tf_op jit(solution)/shard_map/ppermute | solution.py:41
  57.7 3.4 %collective-permute-done.18.refs_0_ = bf16[320,512]{1,0:T(8,128)(2,1)S(1)} collective-permute-done((bf16[320,512]{1,0:T(8,128)(2,1)S(1)}, bf16[320,512]{1,0:T(8,128)(2,1)S(1)}, u32[]{:S(2)}, u32[]{:S(2)}) %collective-permute-start.18) | collective-permute-done | bytes 327712 | tf_op jit(solution)/shard_map/ppermute | solution.py:41
  61.4 2.7 %collective-permute-start.28 = (bf16[256,1280]{1,0:T(8,128)(2,1)S(1)}, bf16[256,1280]{1,0:T(8,128)(2,1)S(1)}, u32[]{:S(2)}, u32[]{:S(2)}) collective-permute-start(bf16[256,1280]{1,0:T(8,128)(2,1)S(1)} %get-tuple-element.214), channel_id=1, source_target_pairs={{0,1},{1,0},{2,3},{3,2},{4,5},{5,4},{6,7},{7,6},{8,9},{9,8},{10,11... | collective-permute-start | bytes 1966088 | tf_op jit(solution)/shard_map/ppermute | solution.py:45
  64.1 2.4 %shard_map.88 = (bf16[256,1280]{1,0:T(8,128)(2,1)S(1)}, bf16[256,1280]{1,0:T(8,128)(2,1)S(1)}, f32[8,128]{1,0:T(8,128)S(1)}) custom-call(bf16[256,1024]{1,0:T(8,128)(2,1)S(1)} %bitcast.21, bf16[256,1024]{1,0:T(8,128)(2,1)S(1)} %get-tuple-element.163.refs_1_.refs_3_, bf16[320,512]{1,0:T(8,128)(2,1)S(1)} %get-tuple-element.177.refs_2_, ...), custom_call_target="tpu_custom_call" | custom-call | flops 1342177280 | tf_op jit(solution)/shard_map/pallas_call | solution.py:77
  66.5 2.2 %collective-permute-start.25 = (bf16[320,512]{1,0:T(8,128)(2,1)S(1)}, bf16[320,512]{1,0:T(8,128)(2,1)S(1)}, u32[]{:S(2)}, u32[]{:S(2)}) collective-permute-start(bf16[320,512]{1,0:T(8,128)(2,1)S(1)} %get-tuple-element.208), channel_id=1, source_target_pairs={{0,14},{1,15},{2,0},{3,1},{4,2},{5,3},{6,4},{7,5},{8,6},{9,7},{10,... | collective-permute-start | bytes 983048 | tf_op jit(solution)/shard_map/ppermute | solution.py:41
  69.5 3.2 %collective-permute-start.30 = (bf16[320,512]{1,0:T(8,128)(2,1)S(1)}, bf16[320,512]{1,0:T(8,128)(2,1)S(1)}, u32[]{:S(2)}, u32[]{:S(2)}) collective-permute-start(bf16[320,512]{1,0:T(8,128)(2,1)S(1)} %get-tuple-element.218), channel_id=1, source_target_pairs={{0,14},{1,15},{2,0},{3,1},{4,2},{5,3},{6,4},{7,5},{8,6},{9,7},{10,... | collective-permute-start | bytes 983048 | tf_op jit(solution)/shard_map/ppermute | solution.py:41
  72.7 2.4 %collective-permute-done.24.refs_1_ = bf16[320,512]{1,0:T(8,128)(2,1)S(1)} collective-permute-done((bf16[320,512]{1,0:T(8,128)(2,1)S(1)}, bf16[320,512]{1,0:T(8,128)(2,1)S(1)}, u32[]{:S(2)}, u32[]{:S(2)}) %collective-permute-start.24) | collective-permute-done | bytes 327712 | tf_op jit(solution)/shard_map/ppermute | solution.py:41
  79.1 3.0 %collective-permute-done.29.refs_1_ = bf16[320,512]{1,0:T(8,128)(2,1)S(1)} collective-permute-done((bf16[320,512]{1,0:T(8,128)(2,1)S(1)}, bf16[320,512]{1,0:T(8,128)(2,1)S(1)}, u32[]{:S(2)}, u32[]{:S(2)}) %collective-permute-start.29) | collective-permute-done | bytes 327712 | tf_op jit(solution)/shard_map/ppermute | solution.py:41
  87.8 2.5 %shard_map.94 = (bf16[256,5120]{1,0:T(8,128)(2,1)}, f32[8,128]{1,0:T(8,128)S(1)}) custom-call(s32[9]{0:T(128)S(1)} %pad_add_fusion.where_ref, bf16[256,1280]{1,0:T(8,128)(2,1)S(1)} %get-tuple-element.213.own_ref, bf16[256,1280]{1,0:T(8,128)(2,1)S(1)} %collective-permute-done.28.arrived_ref, f32[8,128]{1,0:T(8,128)S(1)} %get-tuple-element.223.refs_0_), custom_call_target="tpu_custom_call" | custom-call | bytes 2621440 | tf_op jit(solution)/shard_map/pallas_call | solution.py:234
  90.3 2.4 %collective-permute-done.27.refs_3_ = bf16[320,512]{1,0:T(8,128)(2,1)S(1)} collective-permute-done((bf16[320,512]{1,0:T(8,128)(2,1)S(1)}, bf16[320,512]{1,0:T(8,128)(2,1)S(1)}, u32[]{:S(2)}, u32[]{:S(2)}) %collective-permute-start.27) | collective-permute-done | bytes 327712 | tf_op jit(solution)/shard_map/ppermute | solution.py:41
  93.0 3.2 %collective-permute-start.31 = (bf16[320,512]{1,0:T(8,128)(2,1)S(1)}, bf16[320,512]{1,0:T(8,128)(2,1)S(1)}, u32[]{:S(2)}, u32[]{:S(2)}) collective-permute-start(bf16[320,512]{1,0:T(8,128)(2,1)S(1)} %get-tuple-element.229), channel_id=1, source_target_pairs={{0,14},{1,15},{2,0},{3,1},{4,2},{5,3},{6,4},{7,5},{8,6},{9,7},{10,... | collective-permute-start | bytes 983048 | tf_op jit(solution)/shard_map/ppermute | solution.py:41
  96.1 2.5 %shard_map.96 = (bf16[256,5120]{1,0:T(8,128)(2,1)}, f32[8,128]{1,0:T(8,128)S(1)}) custom-call(s32[9]{0:T(128)S(1)} %pad_add_fusion.where_ref, bf16[256,1280]{1,0:T(8,128)(2,1)S(1)} %get-tuple-element.193.own_ref, bf16[256,1280]{1,0:T(8,128)(2,1)S(1)} %collective-permute-done.20.arrived_ref, ...), custom_call_target="tpu_custom_call", output_to_operand_aliasing={{0}: (4, {})} | custom-call | bytes 2621440 | tf_op jit(solution)/shard_map/pallas_call | solution.py:234
  100.1 3.2 %collective-permute-start.36 = (bf16[320,512]{1,0:T(8,128)(2,1)S(1)}, bf16[320,512]{1,0:T(8,128)(2,1)}, u32[]{:S(2)}, u32[]{:S(2)}) collective-permute-start(bf16[320,512]{1,0:T(8,128)(2,1)S(1)} %get-tuple-element.239), channel_id=1, source_target_pairs={{0,14},{1,15},{2,0},{3,1},{4,2},{5,3},{6,4},{7,5},{8,6},{9,7},{10,... | collective-permute-start | bytes 983048 | tf_op jit(solution)/shard_map/ppermute | solution.py:41
  104.0 2.7 %collective-permute-done.31.refs_1_ = bf16[320,512]{1,0:T(8,128)(2,1)S(1)} collective-permute-done((bf16[320,512]{1,0:T(8,128)(2,1)S(1)}, bf16[320,512]{1,0:T(8,128)(2,1)S(1)}, u32[]{:S(2)}, u32[]{:S(2)}) %collective-permute-start.31) | collective-permute-done | bytes 327712 | tf_op jit(solution)/shard_map/ppermute | solution.py:41
  106.7 2.2 %shard_map.98 = (f32[320,1024]{1,0:T(8,128)S(1)}, f32[320,1024]{1,0:T(8,128)S(1)}, f32[8,128]{1,0:T(8,128)}) custom-call(f32[320,1024]{1,0:T(8,128)S(1)} %get-tuple-element.228.refs_0_, bf16[320,512]{1,0:T(8,128)(2,1)S(1)} %collective-permute-done.31.refs_1_, bf16[320,512]{1,0:T(8,128)(2,1)S(1)} %collective-permute-done.32.refs_2_, f32[320,1024]{1,0:T(8,128)} %bitcast.24, ...), custom_call_target="tpu_custom_call" | custom-call | tf_op jit(solution)/shard_map/pallas_call | solution.py:77
  110.3 1.9 %shard_map.99 = (bf16[320,1024]{1,0:T(8,128)(2,1)S(1)}, f32[8,128]{1,0:T(8,128)}) custom-call(f32[320,1024]{1,0:T(8,128)S(1)} %get-tuple-element.240.refs_0_, bf16[320,512]{1,0:T(8,128)(2,1)} %collective-permute-done.35.refs_1_, bf16[320,512]{1,0:T(8,128)(2,1)} %collective-permute-done.36.refs_2_), custom_call_target="tpu_custom_call" | custom-call | tf_op jit(solution)/shard_map/pallas_call | solution.py:77
  112.3 14.9 %conditional.1 = (f32[320,1024]{1,0:T(8,128)}, f32[1,320,1024]{2,1,0:T(8,128)S(1)}) conditional(s32[]{:T(128)} %clamp.3, (f32[320,1024]{1,0:T(8,128)S(1)}, bf16[320,512]{1,0:T(8,128)(2,1)}, bf16[320,512]{1,0:T(8,128)(2,1)}, f32[320,1024]{1,0:T(8,128)S(1)}, bf16[320,1024]{1,0:T(8,128)(2,1)S(1)}) %tuple.34, ...), branch_computations={%region_0.1_spmd, %region_1.2_spmd, %region_2.3_spmd, %region_3.4_... | conditional | bytes 2621496 | solution.py:459
  112.3 2.1 %collective-permute-start.3 = (bf16[320,1024]{1,0:T(8,128)(2,1)S(1)}, bf16[320,1024]{1,0:T(8,128)(2,1)S(1)}, u32[]{:S(2)}, u32[]{:S(2)}) collective-permute-start(bf16[320,1024]{1,0:T(8,128)(2,1)S(1)} %get-tuple-element.68), channel_id=1, source_target_pairs={{0,128},{16,144},{32,160},{48,176},{64,192},{80,208},{96,224},{112... | collective-permute-start | bytes 1966088 | tf_op jit(solution)/shard_map/cond/branch_3_fun/ppermute | solution.py:50
  114.4 2.4 %branch_3_fun.2 = (f32[320,1024]{1,0:T(8,128)}, f32[320,1024]{1,0:T(8,128)S(1)}, f32[8,128]{1,0:T(8,128)}) custom-call(f32[320,1024]{1,0:T(8,128)S(1)} %get-tuple-element.62.refs_0_, bf16[320,512]{1,0:T(8,128)(2,1)} %get-tuple-element.63.refs_1_, bf16[320,512]{1,0:T(8,128)(2,1)} %get-tuple-element.64.refs_2_, f32[320,1024]{1,0:T(8,128)S(1)} %get-tuple-element.65.refs_3_), custom_call_target="tpu_custom_call" | custom-call | tf_op jit(solution)/shard_map/cond/branch_3_fun/pallas_call | solution.py:77
  116.8 10.1 %collective-permute-done.3.arrived_ref = bf16[320,1024]{1,0:T(8,128)(2,1)S(1)} collective-permute-done((bf16[320,1024]{1,0:T(8,128)(2,1)S(1)}, bf16[320,1024]{1,0:T(8,128)(2,1)S(1)}, u32[]{:S(2)}, u32[]{:S(2)}) %collective-permute-start.3) | collective-permute-done | bytes 655392 | tf_op jit(solution)/shard_map/cond/branch_3_fun/ppermute | solution.py:50
  (77 shorter events, 31.5 us)
Async XLA Ops:
  0.6 27.2 %collective-permute-start.6 = (bf16[256,1024]{1,0:T(8,128)(2,1)}, bf16[256,1024]{1,0:T(8,128)(2,1)S(1)}, u32[]{:S(2)}, u32[]{:S(2)}) collective-permute-start(bf16[256,1024]{1,0:T(8,128)(2,1)} %bitcast.18), channel_id=1, source_target_pairs={{0,1},{1,0},{2,3},{3,2},{4,5},{5,4},{6,7},{7,6},{8,9},{9,8},{10,11... | collective-permute-start | bytes 1572872 | tf_op jit(solution)/shard_map/ppermute | solution.py:45
  4.3 14.4 %collective-permute-start.7 = (bf16[320,512]{1,0:T(8,128)(2,1)S(1)}, bf16[320,512]{1,0:T(8,128)(2,1)S(1)}, u32[]{:S(2)}, u32[]{:S(2)}) collective-permute-start(bf16[320,512]{1,0:T(8,128)(2,1)S(1)} %get-tuple-element.159.refs_7_), channel_id=1, source_target_pairs={{0,2},{1,3},{2,4},{3,5},{4,6},{5,7},{6,8},{7,9},{8,10},{9,11},{10,... | collective-permute-start | bytes 983048 | tf_op jit(solution)/shard_map/ppermute | solution.py:41
  6.2 12.5 %collective-permute-start.8 = (bf16[320,512]{1,0:T(8,128)(2,1)S(1)}, bf16[320,512]{1,0:T(8,128)(2,1)S(1)}, u32[]{:S(2)}, u32[]{:S(2)}) collective-permute-start(bf16[320,512]{1,0:T(8,128)(2,1)S(1)} %get-tuple-element.158.refs_6_), channel_id=1, source_target_pairs={{0,14},{1,15},{2,0},{3,1},{4,2},{5,3},{6,4},{7,5},{8,6},{9,7},{10,... | collective-permute-start | bytes 983048 | tf_op jit(solution)/shard_map/ppermute | solution.py:41
  10.1 15.6 %collective-permute-start.4 = (bf16[320,512]{1,0:T(8,128)(2,1)S(1)}, bf16[320,512]{1,0:T(8,128)(2,1)S(1)}, u32[]{:S(2)}, u32[]{:S(2)}) collective-permute-start(bf16[320,512]{1,0:T(8,128)(2,1)S(1)} %get-tuple-element.158.refs_6_), channel_id=1, source_target_pairs={{0,2},{1,3},{2,4},{3,5},{4,6},{5,7},{6,8},{7,9},{8,10},{9,11},{10,... | collective-permute-start | bytes 983048 | tf_op jit(solution)/shard_map/ppermute | solution.py:41
  10.1 17.6 %collective-permute-start.5 = (bf16[320,512]{1,0:T(8,128)(2,1)S(1)}, bf16[320,512]{1,0:T(8,128)(2,1)S(1)}, u32[]{:S(2)}, u32[]{:S(2)}) collective-permute-start(bf16[320,512]{1,0:T(8,128)(2,1)S(1)} %get-tuple-element.159.refs_7_), channel_id=1, source_target_pairs={{0,14},{1,15},{2,0},{3,1},{4,2},{5,3},{6,4},{7,5},{8,6},{9,7},{10,... | collective-permute-start | bytes 983048 | tf_op jit(solution)/shard_map/ppermute | solution.py:41
  18.8 13.9 %collective-permute-start.9 = (bf16[320,512]{1,0:T(8,128)(2,1)S(1)}, bf16[320,512]{1,0:T(8,128)(2,1)S(1)}, u32[]{:S(2)}, u32[]{:S(2)}) collective-permute-start(bf16[320,512]{1,0:T(8,128)(2,1)S(1)} %get-tuple-element.164.refs_5_), channel_id=1, source_target_pairs={{0,2},{1,3},{2,4},{3,5},{4,6},{5,7},{6,8},{7,9},{8,10},{9,11},{10,... | collective-permute-start | bytes 983048 | tf_op jit(solution)/shard_map/ppermute | solution.py:41
  19.0 13.8 %collective-permute-start.10 = (bf16[320,512]{1,0:T(8,128)(2,1)S(1)}, bf16[320,512]{1,0:T(8,128)(2,1)S(1)}, u32[]{:S(2)}, u32[]{:S(2)}) collective-permute-start(bf16[320,512]{1,0:T(8,128)(2,1)S(1)} %get-tuple-element.165.refs_2_), channel_id=1, source_target_pairs={{0,14},{1,15},{2,0},{3,1},{4,2},{5,3},{6,4},{7,5},{8,6},{9,7},{10,... | collective-permute-start | bytes 983048 | tf_op jit(solution)/shard_map/ppermute | solution.py:41
  25.7 16.0 %collective-permute-start.13 = (bf16[960,256]{1,0:T(8,128)(2,1)S(1)}, bf16[960,256]{1,0:T(8,128)(2,1)S(1)}, u32[]{:S(2)}, u32[]{:S(2)}) collective-permute-start(bf16[960,256]{1,0:T(8,128)(2,1)S(1)} %get-tuple-element.169), channel_id=1, source_target_pairs={{0,1},{1,0},{2,3},{3,2},{4,5},{5,4},{6,7},{7,6},{8,9},{9,8},{10,11... | collective-permute-start | bytes 1474568 | tf_op jit(solution)/shard_map/ppermute | solution.py:45
  28.0 11.9 %collective-permute-start.14 = (bf16[320,512]{1,0:T(8,128)(2,1)S(1)}, bf16[320,512]{1,0:T(8,128)(2,1)S(1)}, u32[]{:S(2)}, u32[]{:S(2)}) collective-permute-start(bf16[320,512]{1,0:T(8,128)(2,1)S(1)} %get-tuple-element.171.refs_4_), channel_id=1, source_target_pairs={{0,2},{1,3},{2,4},{3,5},{4,6},{5,7},{6,8},{7,9},{8,10},{9,11},{10,... | collective-permute-start | bytes 983048 | tf_op jit(solution)/shard_map/ppermute | solution.py:41
  28.1 13.4 %collective-permute-start.15 = (bf16[320,512]{1,0:T(8,128)(2,1)S(1)}, bf16[320,512]{1,0:T(8,128)(2,1)S(1)}, u32[]{:S(2)}, u32[]{:S(2)}) collective-permute-start(bf16[320,512]{1,0:T(8,128)(2,1)S(1)} %get-tuple-element.170.refs_3_), channel_id=1, source_target_pairs={{0,14},{1,15},{2,0},{3,1},{4,2},{5,3},{6,4},{7,5},{8,6},{9,7},{10,... | collective-permute-start | bytes 983048 | tf_op jit(solution)/shard_map/ppermute | solution.py:41
  32.9 14.5 %collective-permute-start.11 = (bf16[320,512]{1,0:T(8,128)(2,1)S(1)}, bf16[320,512]{1,0:T(8,128)(2,1)S(1)}, u32[]{:S(2)}, u32[]{:S(2)}) collective-permute-start(bf16[320,512]{1,0:T(8,128)(2,1)S(1)} %get-tuple-element.167.refs_9_), channel_id=1, source_target_pairs={{0,2},{1,3},{2,4},{3,5},{4,6},{5,7},{6,8},{7,9},{8,10},{9,11},{10,... | collective-permute-start | bytes 983048 | tf_op jit(solution)/shard_map/ppermute | solution.py:41
  33.1 14.3 %collective-permute-start.12 = (bf16[320,512]{1,0:T(8,128)(2,1)S(1)}, bf16[320,512]{1,0:T(8,128)(2,1)S(1)}, u32[]{:S(2)}, u32[]{:S(2)}) collective-permute-start(bf16[320,512]{1,0:T(8,128)(2,1)S(1)} %get-tuple-element.168.refs_6_), channel_id=1, source_target_pairs={{0,14},{1,15},{2,0},{3,1},{4,2},{5,3},{6,4},{7,5},{8,6},{9,7},{10,... | collective-permute-start | bytes 983048 | tf_op jit(solution)/shard_map/ppermute | solution.py:41
  40.0 26.6 %collective-permute-start.21 = (bf16[1600,256]{1,0:T(8,128)(2,1)S(1)}, bf16[1600,256]{1,0:T(8,128)(2,1)S(1)}, u32[]{:S(2)}, u32[]{:S(2)}) collective-permute-start(bf16[1600,256]{1,0:T(8,128)(2,1)S(1)} %get-tuple-element.196), channel_id=1, source_target_pairs={{0,1},{1,0},{2,3},{3,2},{4,5},{5,4},{6,7},{7,6},{8,9},{9,8},{10,11... | collective-permute-start | bytes 2457608 | tf_op jit(solution)/shard_map/ppermute | solution.py:45
  41.7 12.3 %collective-permute-start.16 = (bf16[320,512]{1,0:T(8,128)(2,1)S(1)}, bf16[320,512]{1,0:T(8,128)(2,1)S(1)}, u32[]{:S(2)}, u32[]{:S(2)}) collective-permute-start(bf16[320,512]{1,0:T(8,128)(2,1)S(1)} %get-tuple-element.174.refs_8_), channel_id=1, source_target_pairs={{0,2},{1,3},{2,4},{3,5},{4,6},{5,7},{6,8},{7,9},{8,10},{9,11},{10,... | collective-permute-start | bytes 983048 | tf_op jit(solution)/shard_map/ppermute | solution.py:41
  41.8 12.2 %collective-permute-start.17 = (bf16[320,512]{1,0:T(8,128)(2,1)S(1)}, bf16[320,512]{1,0:T(8,128)(2,1)S(1)}, u32[]{:S(2)}, u32[]{:S(2)}) collective-permute-start(bf16[320,512]{1,0:T(8,128)(2,1)S(1)} %get-tuple-element.173.refs_7_), channel_id=1, source_target_pairs={{0,14},{1,15},{2,0},{3,1},{4,2},{5,3},{6,4},{7,5},{8,6},{9,7},{10,... | collective-permute-start | bytes 983048 | tf_op jit(solution)/shard_map/ppermute | solution.py:41
  47.8 13.3 %collective-permute-start.18 = (bf16[320,512]{1,0:T(8,128)(2,1)S(1)}, bf16[320,512]{1,0:T(8,128)(2,1)S(1)}, u32[]{:S(2)}, u32[]{:S(2)}) collective-permute-start(bf16[320,512]{1,0:T(8,128)(2,1)S(1)} %get-tuple-element.186.refs_5_), channel_id=1, source_target_pairs={{0,2},{1,3},{2,4},{3,5},{4,6},{5,7},{6,8},{7,9},{8,10},{9,11},{10,... | collective-permute-start | bytes 983048 | tf_op jit(solution)/shard_map/ppermute | solution.py:41
  47.9 13.2 %collective-permute-start.19 = (bf16[320,512]{1,0:T(8,128)(2,1)S(1)}, bf16[320,512]{1,0:T(8,128)(2,1)S(1)}, u32[]{:S(2)}, u32[]{:S(2)}) collective-permute-start(bf16[320,512]{1,0:T(8,128)(2,1)S(1)} %get-tuple-element.177.refs_2_), channel_id=1, source_target_pairs={{0,14},{1,15},{2,0},{3,1},{4,2},{5,3},{6,4},{7,5},{8,6},{9,7},{10,... | collective-permute-start | bytes 983048 | tf_op jit(solution)/shard_map/ppermute | solution.py:41
  54.3 14.5 %collective-permute-start.22 = (bf16[320,512]{1,0:T(8,128)(2,1)S(1)}, bf16[320,512]{1,0:T(8,128)(2,1)S(1)}, u32[]{:S(2)}, u32[]{:S(2)}) collective-permute-start(bf16[320,512]{1,0:T(8,128)(2,1)S(1)} %get-tuple-element.198), channel_id=1, source_target_pairs={{0,2},{1,3},{2,4},{3,5},{4,6},{5,7},{6,8},{7,9},{8,10},{9,11},{10,... | collective-permute-start | bytes 983048 | tf_op jit(solution)/shard_map/ppermute | solution.py:41
  54.4 14.4 %collective-permute-start.23 = (bf16[320,512]{1,0:T(8,128)(2,1)S(1)}, bf16[320,512]{1,0:T(8,128)(2,1)S(1)}, u32[]{:S(2)}, u32[]{:S(2)}) collective-permute-start(bf16[320,512]{1,0:T(8,128)(2,1)S(1)} %get-tuple-element.200), channel_id=1, source_target_pairs={{0,14},{1,15},{2,0},{3,1},{4,2},{5,3},{6,4},{7,5},{8,6},{9,7},{10,... | collective-permute-start | bytes 983048 | tf_op jit(solution)/shard_map/ppermute | solution.py:41
  61.3 13.8 %collective-permute-start.24 = (bf16[320,512]{1,0:T(8,128)(2,1)S(1)}, bf16[320,512]{1,0:T(8,128)(2,1)S(1)}, u32[]{:S(2)}, u32[]{:S(2)}) collective-permute-start(bf16[320,512]{1,0:T(8,128)(2,1)S(1)} %get-tuple-element.206), channel_id=1, source_target_pairs={{0,2},{1,3},{2,4},{3,5},{4,6},{5,7},{6,8},{7,9},{8,10},{9,11},{10,... | collective-permute-start | bytes 983048 | tf_op jit(solution)/shard_map/ppermute | solution.py:41
  61.4 24.5 %collective-permute-start.28 = (bf16[256,1280]{1,0:T(8,128)(2,1)S(1)}, bf16[256,1280]{1,0:T(8,128)(2,1)S(1)}, u32[]{:S(2)}, u32[]{:S(2)}) collective-permute-start(bf16[256,1280]{1,0:T(8,128)(2,1)S(1)} %get-tuple-element.214), channel_id=1, source_target_pairs={{0,1},{1,0},{2,3},{3,2},{4,5},{5,4},{6,7},{7,6},{8,9},{9,8},{10,11... | collective-permute-start | bytes 1966088 | tf_op jit(solution)/shard_map/ppermute | solution.py:45
  66.5 12.0 %collective-permute-start.25 = (bf16[320,512]{1,0:T(8,128)(2,1)S(1)}, bf16[320,512]{1,0:T(8,128)(2,1)S(1)}, u32[]{:S(2)}, u32[]{:S(2)}) collective-permute-start(bf16[320,512]{1,0:T(8,128)(2,1)S(1)} %get-tuple-element.208), channel_id=1, source_target_pairs={{0,14},{1,15},{2,0},{3,1},{4,2},{5,3},{6,4},{7,5},{8,6},{9,7},{10,... | collective-permute-start | bytes 983048 | tf_op jit(solution)/shard_map/ppermute | solution.py:41
  69.4 12.7 %collective-permute-start.29 = (bf16[320,512]{1,0:T(8,128)(2,1)S(1)}, bf16[320,512]{1,0:T(8,128)(2,1)S(1)}, u32[]{:S(2)}, u32[]{:S(2)}) collective-permute-start(bf16[320,512]{1,0:T(8,128)(2,1)S(1)} %get-tuple-element.216), channel_id=1, source_target_pairs={{0,2},{1,3},{2,4},{3,5},{4,6},{5,7},{6,8},{7,9},{8,10},{9,11},{10,... | collective-permute-start | bytes 983048 | tf_op jit(solution)/shard_map/ppermute | solution.py:41
  69.5 14.8 %collective-permute-start.30 = (bf16[320,512]{1,0:T(8,128)(2,1)S(1)}, bf16[320,512]{1,0:T(8,128)(2,1)S(1)}, u32[]{:S(2)}, u32[]{:S(2)}) collective-permute-start(bf16[320,512]{1,0:T(8,128)(2,1)S(1)} %get-tuple-element.218), channel_id=1, source_target_pairs={{0,14},{1,15},{2,0},{3,1},{4,2},{5,3},{6,4},{7,5},{8,6},{9,7},{10,... | collective-permute-start | bytes 983048 | tf_op jit(solution)/shard_map/ppermute | solution.py:41
  75.1 21.1 %collective-permute-start.20 = (bf16[256,1280]{1,0:T(8,128)(2,1)S(1)}, bf16[256,1280]{1,0:T(8,128)(2,1)S(1)}, u32[]{:S(2)}, u32[]{:S(2)}) collective-permute-start(bf16[256,1280]{1,0:T(8,128)(2,1)S(1)} %get-tuple-element.194), channel_id=1, source_target_pairs={{0,1},{1,0},{2,3},{3,2},{4,5},{5,4},{6,7},{7,6},{8,9},{9,8},{10,11... | collective-permute-start | bytes 1966088 | tf_op jit(solution)/shard_map/ppermute | solution.py:45
  78.8 11.5 %collective-permute-start.26 = (bf16[320,512]{1,0:T(8,128)(2,1)S(1)}, bf16[320,512]{1,0:T(8,128)(2,1)S(1)}, u32[]{:S(2)}, u32[]{:S(2)}) collective-permute-start(bf16[320,512]{1,0:T(8,128)(2,1)S(1)} %get-tuple-element.210), channel_id=1, source_target_pairs={{0,2},{1,3},{2,4},{3,5},{4,6},{5,7},{6,8},{7,9},{8,10},{9,11},{10,... | collective-permute-start | bytes 983048 | tf_op jit(solution)/shard_map/ppermute | solution.py:41
  82.1 10.6 %collective-permute-start.27 = (bf16[320,512]{1,0:T(8,128)(2,1)S(1)}, bf16[320,512]{1,0:T(8,128)(2,1)S(1)}, u32[]{:S(2)}, u32[]{:S(2)}) collective-permute-start(bf16[320,512]{1,0:T(8,128)(2,1)S(1)} %get-tuple-element.212), channel_id=1, source_target_pairs={{0,14},{1,15},{2,0},{3,1},{4,2},{5,3},{6,4},{7,5},{8,6},{9,7},{10,... | collective-permute-start | bytes 983048 | tf_op jit(solution)/shard_map/ppermute | solution.py:41
  84.5 14.2 %collective-permute-start.33 = (bf16[320,512]{1,0:T(8,128)(2,1)S(1)}, bf16[320,512]{1,0:T(8,128)(2,1)S(1)}, u32[]{:S(2)}, u32[]{:S(2)}) collective-permute-start(bf16[320,512]{1,0:T(8,128)(2,1)S(1)} %get-tuple-element.232), channel_id=1, source_target_pairs={{0,2},{1,3},{2,4},{3,5},{4,6},{5,7},{6,8},{7,9},{8,10},{9,11},{10,... | collective-permute-start | bytes 983048 | tf_op jit(solution)/shard_map/ppermute | solution.py:41
  86.0 13.8 %collective-permute-start.34 = (bf16[320,512]{1,0:T(8,128)(2,1)S(1)}, bf16[320,512]{1,0:T(8,128)(2,1)S(1)}, u32[]{:S(2)}, u32[]{:S(2)}) collective-permute-start(bf16[320,512]{1,0:T(8,128)(2,1)S(1)} %get-tuple-element.234), channel_id=1, source_target_pairs={{0,14},{1,15},{2,0},{3,1},{4,2},{5,3},{6,4},{7,5},{8,6},{9,7},{10,... | collective-permute-start | bytes 983048 | tf_op jit(solution)/shard_map/ppermute | solution.py:41
  93.0 13.7 %collective-permute-start.31 = (bf16[320,512]{1,0:T(8,128)(2,1)S(1)}, bf16[320,512]{1,0:T(8,128)(2,1)S(1)}, u32[]{:S(2)}, u32[]{:S(2)}) collective-permute-start(bf16[320,512]{1,0:T(8,128)(2,1)S(1)} %get-tuple-element.229), channel_id=1, source_target_pairs={{0,14},{1,15},{2,0},{3,1},{4,2},{5,3},{6,4},{7,5},{8,6},{9,7},{10,... | collective-permute-start | bytes 983048 | tf_op jit(solution)/shard_map/ppermute | solution.py:41
  96.1 10.6 %collective-permute-start.32 = (bf16[320,512]{1,0:T(8,128)(2,1)S(1)}, bf16[320,512]{1,0:T(8,128)(2,1)S(1)}, u32[]{:S(2)}, u32[]{:S(2)}) collective-permute-start(bf16[320,512]{1,0:T(8,128)(2,1)S(1)} %get-tuple-element.230), channel_id=1, source_target_pairs={{0,2},{1,3},{2,4},{3,5},{4,6},{5,7},{6,8},{7,9},{8,10},{9,11},{10,... | collective-permute-start | bytes 983048 | tf_op jit(solution)/shard_map/ppermute | solution.py:41
  112.3 14.7 %collective-permute-start.3 = (bf16[320,1024]{1,0:T(8,128)(2,1)S(1)}, bf16[320,1024]{1,0:T(8,128)(2,1)S(1)}, u32[]{:S(2)}, u32[]{:S(2)}) collective-permute-start(bf16[320,1024]{1,0:T(8,128)(2,1)S(1)} %get-tuple-element.68), channel_id=1, source_target_pairs={{0,128},{16,144},{32,160},{48,176},{64,192},{80,208},{96,224},{112... | collective-permute-start | bytes 1966088 | tf_op jit(solution)/shard_map/cond/branch_3_fun/ppermute | solution.py:50
  (8 other events, 59.0 us)
where the time goes:
time: 129 us; the launch traced here: 128 us
  starting transfers between devices  57.1 us (44%)
  waiting for transfers between devices  39.1 us (30%)
  Pallas kernels  27.6 us (21%)
  local copies, waits for them, and re-layouts  2.81 us (2%)
  between operations  1.61 us (1%)
    ppermute x28, starting transfers between devices, along_z(): lax.ppermute(part, 'fsdp', [(i, (i + PAIR * by) % length) for i in range(...  47 us
    ppermute x28, waiting for transfers between devices, along_z(): lax.ppermute(part, 'fsdp', [(i, (i + PAIR * by) % length) for i in range(...  29 us
    pallas_call x21, Pallas kernels, in_vmem(): pl.pallas_call(body, in_specs=[VMEM] * (inputs + len(after)), out_specs=[...  19.5 us
    ppermute x1, waiting for transfers between devices, along_group(): lax.ppermute(part, 'group', [(i, (i + by) % length) for i in range(length)])  10.1 us
    ppermute x5, starting transfers between devices, across_pair(): return lax.ppermute(part, 'fsdp', [(i, i ^ 1) for i in range(RING * PAIR)])  7.94 us
    pallas_call x2, Pallas kernels, join(): pl.pallas_call(kernel, grid_spec=pltpu.PrefetchScalarGridSpec(num_scalar_...  5.04 us
    unnamed x12, local copies, waits for them, and re-layouts  2.81 us
    pallas_call x2, Pallas kernels, split_features(): pl.pallas_call(split_kernel, grid_spec=pltpu.PrefetchScalarGridSpec(num_s...  2.74 us
  transfers between devices with their start and end apart: 34, of which 13 were waited for; matrix products, arithmetic and copies ran while one was open for 0% of the time, Pallas kernels for 20%

commit v1 on v0

--- a/solution.py
+++ b/solution.py
@@ -261,9 +261,17 @@
             left_ref[tile, :] = weights_ref[tile, :half].astype(BF16)
             right_ref[tile, :] = weights_ref[tile, half:].astype(BF16)
 
-        by_tiles(rows, short)
-
-    return in_vmem(kernel, [weights], (), [((rows, half), BF16)] * 2)[:2]
+        by_tiles(rows // 2, short)
+
+    return pl.pallas_call(
+        kernel,
+        grid=(2,),
+        in_specs=[pl.BlockSpec((rows // 2, width), lambda i: (i, 0))],
+        out_specs=[pl.BlockSpec((rows // 2, half), lambda i: (i, 0))] * 2,
+        out_shape=[jax.ShapeDtypeStruct((rows, half), BF16)] * 2,
+        compiler_params=PARAMS,
+        cost_estimate=cost(0, 0),
+    )(weights)
 
 
 def settle(own, moment, count, after):
@@ -302,17 +310,20 @@
     rows, width = stepped.shape
     half = width // 2
 
-    def kernel(stepped_ref, left_ref, right_ref, out_ref):
+    def kernel(stepped_ref, left_ref, right_ref, out_ref, *kept_refs):
         for j, arrived_ref in enumerate((left_ref, right_ref)):
             cut = slice(j * half, (j + 1) * half)
 
-            def add(tile, cut=cut, arrived_ref=arrived_ref):
+            def add(tile, cut=cut, arrived_ref=arrived_ref, kept_ref=kept_refs[j]):
+                kept_ref[tile, :] = arrived_ref[tile, :]
                 last = arrived_ref[tile, :].astype(F32) / count
                 out_ref[tile, cut] = (stepped_ref[tile, cut] - 0.5 * last).astype(BF16)
 
             by_tiles(rows, add)
 
-    return in_vmem(kernel, [stepped, *arrived], (), [((rows, width), BF16)])[0]
+    outs = [((rows, width), BF16), *[((rows, half), BF16)] * 2]
+    short, left, right, _ = in_vmem(kernel, [stepped, *arrived], (), outs)
+    return short, (left, right)
 
 
 def mix(stepped, arrived):
@@ -454,7 +465,7 @@
     early = [flying[1, "sa3"], flying[0, "sb3"]]
     settled, stepped, _ = fold(settled, early, weights, count, after)
     arrived = [flying[0, "sa4"], flying[1, "sb4"]]
-    short = stepped_short(stepped, arrived, count)
+    short, arrived = stepped_short(stepped, arrived, count)
     branches = [partial(finish, by=by, count=count) for by in hops]
     new_params, momentum = lax.switch(level, branches, short, settled, arrived, weights)
     return input_grad, new_params, momentum

time: 129 us -> 126 us (0.977); the launches traced: 128 us -> 127 us
  Pallas kernels: 27.6 us -> 25.7 us
    pallas_call x21 -> x20, Pallas kernels: 19.5 us -> 16.2 us  [in_vmem(): pl.pallas_call(body, in_specs=[VMEM] * (inputs + len(after)), out_specs=[...]
    ppermute x1, waiting for transfers between devices: 10.1 us -> 11.6 us  [along_group(): lax.ppermute(part, 'group', [(i, (i + by) % length) for i in range(length)])]
    pallas_call x0 -> x1, Pallas kernels: none -> 1.35 us  [shorten(): pl.pallas_call(kernel, grid=(2,), in_specs=[pl.BlockSpec((rows // 2, widt...]
  transfers between devices with their start and end apart: 34 -> 34, of which waited for: 13 -> 14; matrix products, arithmetic and copies ran while one was open for 0% -> 0% of each run, Pallas kernels for 20% -> 19%
where the time goes in v1:
time: 126 us; the launch traced here: 127 us
  starting transfers between devices  57.8 us (46%)
  waiting for transfers between devices  39.5 us (31%)
  Pallas kernels  25.7 us (20%)
  local copies, waits for them, and re-layouts  2.81 us (2%)
  between operations  1.61 us (1%)
    ppermute x28, starting transfers between devices, along_z(): lax.ppermute(part, 'fsdp', [(i, (i + PAIR * by) % length) for i in range(...  47.2 us
    ppermute x28, waiting for transfers between devices, along_z(): lax.ppermute(part, 'fsdp', [(i, (i + PAIR * by) % length) for i in range(...  27.9 us
    pallas_call x20, Pallas kernels, in_vmem(): pl.pallas_call(body, in_specs=[VMEM] * (inputs + len(after)), out_specs=[...  16.2 us
    ppermute x1, waiting for transfers between devices, along_group(): lax.ppermute(part, 'group', [(i, (i + by) % length) for i in range(length)])  11.6 us
    ppermute x5, starting transfers between devices, across_pair(): return lax.ppermute(part, 'fsdp', [(i, i ^ 1) for i in range(RING * PAIR)])  7.94 us
    pallas_call x2, Pallas kernels, join(): pl.pallas_call(kernel, grid_spec=pltpu.PrefetchScalarGridSpec(num_scalar_...  5.04 us
    unnamed x12, local copies, waits for them, and re-layouts  2.81 us
    pallas_call x2, Pallas kernels, split_features(): pl.pallas_call(split_kernel, grid_spec=pltpu.PrefetchScalarGridSpec(num_s...  2.74 us
  transfers between devices with their start and end apart: 34, of which 14 were waited for; matrix products, arithmetic and copies ran while one was open for 0% of the time, Pallas kernels for 19%

profile of v1, /device:TPU:2, one launch (start us, length us, event | category | flops | bytes accessed | tf_op | source)
XLA Modules:
  0.0 127.5 jit_solution(2298764709688667641)
XLA Ops:
  3.6 2.0 %collective-permute-start.7 = (bf16[320,512]{1,0:T(8,128)(2,1)S(1)}, bf16[320,512]{1,0:T(8,128)(2,1)S(1)}, u32[]{:S(2)}, u32[]{:S(2)}) collective-permute-start(bf16[320,512]{1,0:T(8,128)(2,1)S(1)} %get-tuple-element.161.refs_7_), channel_id=1, source_target_pairs={{0,2},{1,3},{2,4},{3,5},{4,6},{5,7},{6,8},{7,9},{8,10},{9,11},{10,... | collective-permute-start | bytes 983048 | tf_op jit(solution)/shard_map/ppermute | solution.py:41
  5.6 4.0 %collective-permute-start.8 = (bf16[320,512]{1,0:T(8,128)(2,1)S(1)}, bf16[320,512]{1,0:T(8,128)(2,1)S(1)}, u32[]{:S(2)}, u32[]{:S(2)}) collective-permute-start(bf16[320,512]{1,0:T(8,128)(2,1)S(1)} %get-tuple-element.160.refs_6_), channel_id=1, source_target_pairs={{0,14},{1,15},{2,0},{3,1},{4,2},{5,3},{6,4},{7,5},{8,6},{9,7},{10,... | collective-permute-start | bytes 983048 | tf_op jit(solution)/shard_map/ppermute | solution.py:41
  9.7 3.2 %collective-permute-start.5 = (bf16[320,512]{1,0:T(8,128)(2,1)S(1)}, bf16[320,512]{1,0:T(8,128)(2,1)S(1)}, u32[]{:S(2)}, u32[]{:S(2)}) collective-permute-start(bf16[320,512]{1,0:T(8,128)(2,1)S(1)} %get-tuple-element.161.refs_7_), channel_id=1, source_target_pairs={{0,14},{1,15},{2,0},{3,1},{4,2},{5,3},{6,4},{7,5},{8,6},{9,7},{10,... | collective-permute-start | bytes 983048 | tf_op jit(solution)/shard_map/ppermute | solution.py:41
  15.9 2.2 %collective-permute-done.7.refs_0_ = bf16[320,512]{1,0:T(8,128)(2,1)S(1)} collective-permute-done((bf16[320,512]{1,0:T(8,128)(2,1)S(1)}, bf16[320,512]{1,0:T(8,128)(2,1)S(1)}, u32[]{:S(2)}, u32[]{:S(2)}) %collective-permute-start.7) | collective-permute-done | bytes 327712 | tf_op jit(solution)/shard_map/ppermute | solution.py:41
  18.4 3.4 %collective-permute-start.10 = (bf16[320,512]{1,0:T(8,128)(2,1)S(1)}, bf16[320,512]{1,0:T(8,128)(2,1)S(1)}, u32[]{:S(2)}, u32[]{:S(2)}) collective-permute-start(bf16[320,512]{1,0:T(8,128)(2,1)S(1)} %get-tuple-element.167.refs_2_), channel_id=1, source_target_pairs={{0,14},{1,15},{2,0},{3,1},{4,2},{5,3},{6,4},{7,5},{8,6},{9,7},{10,... | collective-permute-start | bytes 983048 | tf_op jit(solution)/shard_map/ppermute | solution.py:41
  21.8 3.4 %collective-permute-done.4.refs_0_ = bf16[320,512]{1,0:T(8,128)(2,1)S(1)} collective-permute-done((bf16[320,512]{1,0:T(8,128)(2,1)S(1)}, bf16[320,512]{1,0:T(8,128)(2,1)S(1)}, u32[]{:S(2)}, u32[]{:S(2)}) %collective-permute-start.4) | collective-permute-done | bytes 327712 | tf_op jit(solution)/shard_map/ppermute | solution.py:41
  27.6 3.2 %collective-permute-start.15 = (bf16[320,512]{1,0:T(8,128)(2,1)S(1)}, bf16[320,512]{1,0:T(8,128)(2,1)S(1)}, u32[]{:S(2)}, u32[]{:S(2)}) collective-permute-start(bf16[320,512]{1,0:T(8,128)(2,1)S(1)} %get-tuple-element.172.refs_3_), channel_id=1, source_target_pairs={{0,14},{1,15},{2,0},{3,1},{4,2},{5,3},{6,4},{7,5},{8,6},{9,7},{10,... | collective-permute-start | bytes 983048 | tf_op jit(solution)/shard_map/ppermute | solution.py:41
  32.5 3.3 %collective-permute-start.12 = (bf16[320,512]{1,0:T(8,128)(2,1)S(1)}, bf16[320,512]{1,0:T(8,128)(2,1)S(1)}, u32[]{:S(2)}, u32[]{:S(2)}) collective-permute-start(bf16[320,512]{1,0:T(8,128)(2,1)S(1)} %get-tuple-element.170.refs_6_), channel_id=1, source_target_pairs={{0,14},{1,15},{2,0},{3,1},{4,2},{5,3},{6,4},{7,5},{8,6},{9,7},{10,... | collective-permute-start | bytes 983048 | tf_op jit(solution)/shard_map/ppermute | solution.py:41
  35.8 3.6 %collective-permute-done.14.refs_0_ = bf16[320,512]{1,0:T(8,128)(2,1)S(1)} collective-permute-done((bf16[320,512]{1,0:T(8,128)(2,1)S(1)}, bf16[320,512]{1,0:T(8,128)(2,1)S(1)}, u32[]{:S(2)}, u32[]{:S(2)}) %collective-permute-start.14) | collective-permute-done | bytes 327712 | tf_op jit(solution)/shard_map/ppermute | solution.py:41
  41.2 3.2 %collective-permute-start.17 = (bf16[320,512]{1,0:T(8,128)(2,1)S(1)}, bf16[320,512]{1,0:T(8,128)(2,1)S(1)}, u32[]{:S(2)}, u32[]{:S(2)}) collective-permute-start(bf16[320,512]{1,0:T(8,128)(2,1)S(1)} %get-tuple-element.175.refs_7_), channel_id=1, source_target_pairs={{0,14},{1,15},{2,0},{3,1},{4,2},{5,3},{6,4},{7,5},{8,6},{9,7},{10,... | collective-permute-start | bytes 983048 | tf_op jit(solution)/shard_map/ppermute | solution.py:41
  44.4 2.4 %shard_map.83 = (bf16[256,1280]{1,0:T(8,128)(2,1)S(1)}, bf16[256,1280]{1,0:T(8,128)(2,1)S(1)}, f32[8,128]{1,0:T(8,128)S(1)}) custom-call(bf16[256,1024]{1,0:T(8,128)(2,1)S(1)} %bitcast.19, bf16[256,1024]{1,0:T(8,128)(2,1)S(1)} %get-tuple-element.165.refs_1_.refs_3_, bf16[320,512]{1,0:T(8,128)(2,1)S(1)} %get-tuple-element.167.refs_2_, ...), custom_call_target="tpu_custom_call" | custom-call | flops 1342177280 | tf_op jit(solution)/shard_map/pallas_call | solution.py:77
  47.3 3.2 %collective-permute-start.19 = (bf16[320,512]{1,0:T(8,128)(2,1)S(1)}, bf16[320,512]{1,0:T(8,128)(2,1)S(1)}, u32[]{:S(2)}, u32[]{:S(2)}) collective-permute-start(bf16[320,512]{1,0:T(8,128)(2,1)S(1)} %get-tuple-element.179.refs_2_), channel_id=1, source_target_pairs={{0,14},{1,15},{2,0},{3,1},{4,2},{5,3},{6,4},{7,5},{8,6},{9,7},{10,... | collective-permute-start | bytes 983048 | tf_op jit(solution)/shard_map/ppermute | solution.py:41
  53.8 3.3 %collective-permute-start.23 = (bf16[320,512]{1,0:T(8,128)(2,1)S(1)}, bf16[320,512]{1,0:T(8,128)(2,1)S(1)}, u32[]{:S(2)}, u32[]{:S(2)}) collective-permute-start(bf16[320,512]{1,0:T(8,128)(2,1)S(1)} %get-tuple-element.202), channel_id=1, source_target_pairs={{0,14},{1,15},{2,0},{3,1},{4,2},{5,3},{6,4},{7,5},{8,6},{9,7},{10,... | collective-permute-start | bytes 983048 | tf_op jit(solution)/shard_map/ppermute | solution.py:41
  57.1 3.4 %collective-permute-done.18.refs_0_ = bf16[320,512]{1,0:T(8,128)(2,1)S(1)} collective-permute-done((bf16[320,512]{1,0:T(8,128)(2,1)S(1)}, bf16[320,512]{1,0:T(8,128)(2,1)S(1)}, u32[]{:S(2)}, u32[]{:S(2)}) %collective-permute-start.18) | collective-permute-done | bytes 327712 | tf_op jit(solution)/shard_map/ppermute | solution.py:41
  60.9 2.7 %collective-permute-start.28 = (bf16[256,1280]{1,0:T(8,128)(2,1)S(1)}, bf16[256,1280]{1,0:T(8,128)(2,1)S(1)}, u32[]{:S(2)}, u32[]{:S(2)}) collective-permute-start(bf16[256,1280]{1,0:T(8,128)(2,1)S(1)} %get-tuple-element.216), channel_id=1, source_target_pairs={{0,1},{1,0},{2,3},{3,2},{4,5},{5,4},{6,7},{7,6},{8,9},{9,8},{10,11... | collective-permute-start | bytes 1966088 | tf_op jit(solution)/shard_map/ppermute | solution.py:45
  63.6 2.4 %shard_map.88 = (bf16[256,1280]{1,0:T(8,128)(2,1)S(1)}, bf16[256,1280]{1,0:T(8,128)(2,1)S(1)}, f32[8,128]{1,0:T(8,128)S(1)}) custom-call(bf16[256,1024]{1,0:T(8,128)(2,1)S(1)} %bitcast.21, bf16[256,1024]{1,0:T(8,128)(2,1)S(1)} %get-tuple-element.165.refs_1_.refs_3_, bf16[320,512]{1,0:T(8,128)(2,1)S(1)} %get-tuple-element.179.refs_2_, ...), custom_call_target="tpu_custom_call" | custom-call | flops 1342177280 | tf_op jit(solution)/shard_map/pallas_call | solution.py:77
  66.0 2.2 %collective-permute-start.25 = (bf16[320,512]{1,0:T(8,128)(2,1)S(1)}, bf16[320,512]{1,0:T(8,128)(2,1)S(1)}, u32[]{:S(2)}, u32[]{:S(2)}) collective-permute-start(bf16[320,512]{1,0:T(8,128)(2,1)S(1)} %get-tuple-element.210), channel_id=1, source_target_pairs={{0,14},{1,15},{2,0},{3,1},{4,2},{5,3},{6,4},{7,5},{8,6},{9,7},{10,... | collective-permute-start | bytes 983048 | tf_op jit(solution)/shard_map/ppermute | solution.py:41
  68.9 3.2 %collective-permute-start.30 = (bf16[320,512]{1,0:T(8,128)(2,1)S(1)}, bf16[320,512]{1,0:T(8,128)(2,1)S(1)}, u32[]{:S(2)}, u32[]{:S(2)}) collective-permute-start(bf16[320,512]{1,0:T(8,128)(2,1)S(1)} %get-tuple-element.220), channel_id=1, source_target_pairs={{0,14},{1,15},{2,0},{3,1},{4,2},{5,3},{6,4},{7,5},{8,6},{9,7},{10,... | collective-permute-start | bytes 983048 | tf_op jit(solution)/shard_map/ppermute | solution.py:41
  72.1 2.4 %collective-permute-done.24.refs_1_ = bf16[320,512]{1,0:T(8,128)(2,1)S(1)} collective-permute-done((bf16[320,512]{1,0:T(8,128)(2,1)S(1)}, bf16[320,512]{1,0:T(8,128)(2,1)S(1)}, u32[]{:S(2)}, u32[]{:S(2)}) %collective-permute-start.24) | collective-permute-done | bytes 327712 | tf_op jit(solution)/shard_map/ppermute | solution.py:41
  76.1 1.9 %shard_map.90 = (f32[320,512]{1,0:T(8,128)S(1)}, f32[320,512]{1,0:T(8,128)S(1)}, f32[320,512]{1,0:T(8,128)S(1)}, f32[320,512]{1,0:T(8,128)S(1)}, f32[320,512]{1,...) custom-call(bf16[1600,256]{1,0:T(8,128)(2,1)S(1)} %get-tuple-element, ...), custom_call_target="tpu_custom_call" | custom-call | flops 1677721600 | tf_op jit(solution)/shard_map/pallas_call | solution.py:77
  78.6 3.0 %collective-permute-done.29.refs_1_ = bf16[320,512]{1,0:T(8,128)(2,1)S(1)} collective-permute-done((bf16[320,512]{1,0:T(8,128)(2,1)S(1)}, bf16[320,512]{1,0:T(8,128)(2,1)S(1)}, u32[]{:S(2)}, u32[]{:S(2)}) %collective-permute-start.29) | collective-permute-done | bytes 327712 | tf_op jit(solution)/shard_map/ppermute | solution.py:41
  81.5 1.9 %collective-permute-start.27 = (bf16[320,512]{1,0:T(8,128)(2,1)S(1)}, bf16[320,512]{1,0:T(8,128)(2,1)S(1)}, u32[]{:S(2)}, u32[]{:S(2)}) collective-permute-start(bf16[320,512]{1,0:T(8,128)(2,1)S(1)} %get-tuple-element.214), channel_id=1, source_target_pairs={{0,14},{1,15},{2,0},{3,1},{4,2},{5,3},{6,4},{7,5},{8,6},{9,7},{10,... | collective-permute-start | bytes 983048 | tf_op jit(solution)/shard_map/ppermute | solution.py:41
  87.2 2.5 %shard_map.94 = (bf16[256,5120]{1,0:T(8,128)(2,1)}, f32[8,128]{1,0:T(8,128)S(1)}) custom-call(s32[9]{0:T(128)S(1)} %pad_add_fusion.where_ref, bf16[256,1280]{1,0:T(8,128)(2,1)S(1)} %get-tuple-element.215.own_ref, bf16[256,1280]{1,0:T(8,128)(2,1)S(1)} %collective-permute-done.28.arrived_ref, f32[8,128]{1,0:T(8,128)S(1)} %get-tuple-element.225.refs_0_), custom_call_target="tpu_custom_call" | custom-call | bytes 2621440 | tf_op jit(solution)/shard_map/pallas_call | solution.py:234
  89.7 2.5 %collective-permute-done.27.refs_3_ = bf16[320,512]{1,0:T(8,128)(2,1)S(1)} collective-permute-done((bf16[320,512]{1,0:T(8,128)(2,1)S(1)}, bf16[320,512]{1,0:T(8,128)(2,1)S(1)}, u32[]{:S(2)}, u32[]{:S(2)}) %collective-permute-start.27) | collective-permute-done | bytes 327712 | tf_op jit(solution)/shard_map/ppermute | solution.py:41
  92.4 3.2 %collective-permute-start.31 = (bf16[320,512]{1,0:T(8,128)(2,1)S(1)}, bf16[320,512]{1,0:T(8,128)(2,1)S(1)}, u32[]{:S(2)}, u32[]{:S(2)}) collective-permute-start(bf16[320,512]{1,0:T(8,128)(2,1)S(1)} %get-tuple-element.231), channel_id=1, source_target_pairs={{0,14},{1,15},{2,0},{3,1},{4,2},{5,3},{6,4},{7,5},{8,6},{9,7},{10,... | collective-permute-start | bytes 983048 | tf_op jit(solution)/shard_map/ppermute | solution.py:41
  95.6 2.5 %shard_map.96 = (bf16[256,5120]{1,0:T(8,128)(2,1)}, f32[8,128]{1,0:T(8,128)S(1)}) custom-call(s32[9]{0:T(128)S(1)} %pad_add_fusion.where_ref, bf16[256,1280]{1,0:T(8,128)(2,1)S(1)} %get-tuple-element.195.own_ref, bf16[256,1280]{1,0:T(8,128)(2,1)S(1)} %collective-permute-done.20.arrived_ref, ...), custom_call_target="tpu_custom_call", output_to_operand_aliasing={{0}: (4, {})} | custom-call | bytes 2621440 | tf_op jit(solution)/shard_map/pallas_call | solution.py:234
  100.3 3.2 %collective-permute-start.36 = (bf16[320,512]{1,0:T(8,128)(2,1)}, bf16[320,512]{1,0:T(8,128)(2,1)S(1)}, u32[]{:S(2)}, u32[]{:S(2)}) collective-permute-start(bf16[320,512]{1,0:T(8,128)(2,1)} %get-tuple-element.242), channel_id=1, source_target_pairs={{0,14},{1,15},{2,0},{3,1},{4,2},{5,3},{6,4},{7,5},{8,6},{9,7},{10,... | collective-permute-start | bytes 983048 | tf_op jit(solution)/shard_map/ppermute | solution.py:41
  104.2 2.0 %collective-permute-done.31.refs_1_ = bf16[320,512]{1,0:T(8,128)(2,1)S(1)} collective-permute-done((bf16[320,512]{1,0:T(8,128)(2,1)S(1)}, bf16[320,512]{1,0:T(8,128)(2,1)S(1)}, u32[]{:S(2)}, u32[]{:S(2)}) %collective-permute-start.31) | collective-permute-done | bytes 327712 | tf_op jit(solution)/shard_map/ppermute | solution.py:41
  106.2 2.2 %shard_map.98 = (f32[320,1024]{1,0:T(8,128)S(1)}, f32[320,1024]{1,0:T(8,128)S(1)}, f32[8,128]{1,0:T(8,128)}) custom-call(f32[320,1024]{1,0:T(8,128)S(1)} %get-tuple-element.230.refs_0_, bf16[320,512]{1,0:T(8,128)(2,1)S(1)} %collective-permute-done.31.refs_1_, bf16[320,512]{1,0:T(8,128)(2,1)S(1)} %collective-permute-done.32.refs_2_, f32[320,1024]{1,0:T(8,128)} %bitcast.24, ...), custom_call_target="tpu_custom_call" | custom-call | tf_op jit(solution)/shard_map/pallas_call | solution.py:77
  110.6 15.9 %conditional.1 = (f32[320,1024]{1,0:T(8,128)}, f32[1,320,1024]{2,1,0:T(8,128)S(1)}) conditional(s32[]{:T(128)} %clamp.3, (f32[320,1024]{1,0:T(8,128)S(1)}, bf16[320,512]{1,0:T(8,128)(2,1)S(1)}, bf16[320,512]{1,0:T(8,128)(2,1)S(1)}, f32[320,1024]{1,0:T(8,128)S(1)}, bf16[320,1024]{1,0:T(8,128)(2,1)S(1)}) %tuple.34, ...), branch_computations={%region_0.1_spmd, %region_1.2_spmd, %region_2.3_spmd, %region_3.4_... | conditional | bytes 2621496 | solution.py:470
  110.6 2.6 %collective-permute-start.1 = (bf16[320,1024]{1,0:T(8,128)(2,1)S(1)}, bf16[320,1024]{1,0:T(8,128)(2,1)S(1)}, u32[]{:S(2)}, u32[]{:S(2)}) collective-permute-start(bf16[320,1024]{1,0:T(8,128)(2,1)S(1)} %get-tuple-element.54), channel_id=1, source_target_pairs={{0,32},{16,48},{32,64},{48,80},{64,96},{80,112},{96,128},{112,144}... | collective-permute-start | bytes 1966088 | tf_op jit(solution)/shard_map/cond/branch_1_fun/ppermute | solution.py:50
  114.5 11.6 %collective-permute-done.1.arrived_ref = bf16[320,1024]{1,0:T(8,128)(2,1)S(1)} collective-permute-done((bf16[320,1024]{1,0:T(8,128)(2,1)S(1)}, bf16[320,1024]{1,0:T(8,128)(2,1)S(1)}, u32[]{:S(2)}, u32[]{:S(2)}) %collective-permute-start.1) | collective-permute-done | bytes 655392 | tf_op jit(solution)/shard_map/cond/branch_1_fun/ppermute | solution.py:50
  (77 shorter events, 30.0 us)
Async XLA Ops:
  0.6 26.6 %collective-permute-start.6 = (bf16[256,1024]{1,0:T(8,128)(2,1)}, bf16[256,1024]{1,0:T(8,128)(2,1)S(1)}, u32[]{:S(2)}, u32[]{:S(2)}) collective-permute-start(bf16[256,1024]{1,0:T(8,128)(2,1)} %bitcast.18), channel_id=1, source_target_pairs={{0,1},{1,0},{2,3},{3,2},{4,5},{5,4},{6,7},{7,6},{8,9},{9,8},{10,11... | collective-permute-start | bytes 1572872 | tf_op jit(solution)/shard_map/ppermute | solution.py:45
  3.6 14.5 %collective-permute-start.7 = (bf16[320,512]{1,0:T(8,128)(2,1)S(1)}, bf16[320,512]{1,0:T(8,128)(2,1)S(1)}, u32[]{:S(2)}, u32[]{:S(2)}) collective-permute-start(bf16[320,512]{1,0:T(8,128)(2,1)S(1)} %get-tuple-element.161.refs_7_), channel_id=1, source_target_pairs={{0,2},{1,3},{2,4},{3,5},{4,6},{5,7},{6,8},{7,9},{8,10},{9,11},{10,... | collective-permute-start | bytes 983048 | tf_op jit(solution)/shard_map/ppermute | solution.py:41
  5.6 12.5 %collective-permute-start.8 = (bf16[320,512]{1,0:T(8,128)(2,1)S(1)}, bf16[320,512]{1,0:T(8,128)(2,1)S(1)}, u32[]{:S(2)}, u32[]{:S(2)}) collective-permute-start(bf16[320,512]{1,0:T(8,128)(2,1)S(1)} %get-tuple-element.160.refs_6_), channel_id=1, source_target_pairs={{0,14},{1,15},{2,0},{3,1},{4,2},{5,3},{6,4},{7,5},{8,6},{9,7},{10,... | collective-permute-start | bytes 983048 | tf_op jit(solution)/shard_map/ppermute | solution.py:41
  9.7 15.5 %collective-permute-start.4 = (bf16[320,512]{1,0:T(8,128)(2,1)S(1)}, bf16[320,512]{1,0:T(8,128)(2,1)S(1)}, u32[]{:S(2)}, u32[]{:S(2)}) collective-permute-start(bf16[320,512]{1,0:T(8,128)(2,1)S(1)} %get-tuple-element.160.refs_6_), channel_id=1, source_target_pairs={{0,2},{1,3},{2,4},{3,5},{4,6},{5,7},{6,8},{7,9},{8,10},{9,11},{10,... | collective-permute-start | bytes 983048 | tf_op jit(solution)/shard_map/ppermute | solution.py:41
  9.7 17.6 %collective-permute-start.5 = (bf16[320,512]{1,0:T(8,128)(2,1)S(1)}, bf16[320,512]{1,0:T(8,128)(2,1)S(1)}, u32[]{:S(2)}, u32[]{:S(2)}) collective-permute-start(bf16[320,512]{1,0:T(8,128)(2,1)S(1)} %get-tuple-element.161.refs_7_), channel_id=1, source_target_pairs={{0,14},{1,15},{2,0},{3,1},{4,2},{5,3},{6,4},{7,5},{8,6},{9,7},{10,... | collective-permute-start | bytes 983048 | tf_op jit(solution)/shard_map/ppermute | solution.py:41
  18.3 13.9 %collective-permute-start.9 = (bf16[320,512]{1,0:T(8,128)(2,1)S(1)}, bf16[320,512]{1,0:T(8,128)(2,1)S(1)}, u32[]{:S(2)}, u32[]{:S(2)}) collective-permute-start(bf16[320,512]{1,0:T(8,128)(2,1)S(1)} %get-tuple-element.166.refs_5_), channel_id=1, source_target_pairs={{0,2},{1,3},{2,4},{3,5},{4,6},{5,7},{6,8},{7,9},{8,10},{9,11},{10,... | collective-permute-start | bytes 983048 | tf_op jit(solution)/shard_map/ppermute | solution.py:41
  18.4 13.8 %collective-permute-start.10 = (bf16[320,512]{1,0:T(8,128)(2,1)S(1)}, bf16[320,512]{1,0:T(8,128)(2,1)S(1)}, u32[]{:S(2)}, u32[]{:S(2)}) collective-permute-start(bf16[320,512]{1,0:T(8,128)(2,1)S(1)} %get-tuple-element.167.refs_2_), channel_id=1, source_target_pairs={{0,14},{1,15},{2,0},{3,1},{4,2},{5,3},{6,4},{7,5},{8,6},{9,7},{10,... | collective-permute-start | bytes 983048 | tf_op jit(solution)/shard_map/ppermute | solution.py:41
  25.2 16.0 %collective-permute-start.13 = (bf16[960,256]{1,0:T(8,128)(2,1)S(1)}, bf16[960,256]{1,0:T(8,128)(2,1)S(1)}, u32[]{:S(2)}, u32[]{:S(2)}) collective-permute-start(bf16[960,256]{1,0:T(8,128)(2,1)S(1)} %get-tuple-element.171), channel_id=1, source_target_pairs={{0,1},{1,0},{2,3},{3,2},{4,5},{5,4},{6,7},{7,6},{8,9},{9,8},{10,11... | collective-permute-start | bytes 1474568 | tf_op jit(solution)/shard_map/ppermute | solution.py:45
  27.5 11.9 %collective-permute-start.14 = (bf16[320,512]{1,0:T(8,128)(2,1)S(1)}, bf16[320,512]{1,0:T(8,128)(2,1)S(1)}, u32[]{:S(2)}, u32[]{:S(2)}) collective-permute-start(bf16[320,512]{1,0:T(8,128)(2,1)S(1)} %get-tuple-element.173.refs_4_), channel_id=1, source_target_pairs={{0,2},{1,3},{2,4},{3,5},{4,6},{5,7},{6,8},{7,9},{8,10},{9,11},{10,... | collective-permute-start | bytes 983048 | tf_op jit(solution)/shard_map/ppermute | solution.py:41
  27.6 13.4 %collective-permute-start.15 = (bf16[320,512]{1,0:T(8,128)(2,1)S(1)}, bf16[320,512]{1,0:T(8,128)(2,1)S(1)}, u32[]{:S(2)}, u32[]{:S(2)}) collective-permute-start(bf16[320,512]{1,0:T(8,128)(2,1)S(1)} %get-tuple-element.172.refs_3_), channel_id=1, source_target_pairs={{0,14},{1,15},{2,0},{3,1},{4,2},{5,3},{6,4},{7,5},{8,6},{9,7},{10,... | collective-permute-start | bytes 983048 | tf_op jit(solution)/shard_map/ppermute | solution.py:41
  32.3 14.5 %collective-permute-start.11 = (bf16[320,512]{1,0:T(8,128)(2,1)S(1)}, bf16[320,512]{1,0:T(8,128)(2,1)S(1)}, u32[]{:S(2)}, u32[]{:S(2)}) collective-permute-start(bf16[320,512]{1,0:T(8,128)(2,1)S(1)} %get-tuple-element.169.refs_9_), channel_id=1, source_target_pairs={{0,2},{1,3},{2,4},{3,5},{4,6},{5,7},{6,8},{7,9},{8,10},{9,11},{10,... | collective-permute-start | bytes 983048 | tf_op jit(solution)/shard_map/ppermute | solution.py:41
  32.5 14.3 %collective-permute-start.12 = (bf16[320,512]{1,0:T(8,128)(2,1)S(1)}, bf16[320,512]{1,0:T(8,128)(2,1)S(1)}, u32[]{:S(2)}, u32[]{:S(2)}) collective-permute-start(bf16[320,512]{1,0:T(8,128)(2,1)S(1)} %get-tuple-element.170.refs_6_), channel_id=1, source_target_pairs={{0,14},{1,15},{2,0},{3,1},{4,2},{5,3},{6,4},{7,5},{8,6},{9,7},{10,... | collective-permute-start | bytes 983048 | tf_op jit(solution)/shard_map/ppermute | solution.py:41
  39.4 26.6 %collective-permute-start.21 = (bf16[1600,256]{1,0:T(8,128)(2,1)S(1)}, bf16[1600,256]{1,0:T(8,128)(2,1)S(1)}, u32[]{:S(2)}, u32[]{:S(2)}) collective-permute-start(bf16[1600,256]{1,0:T(8,128)(2,1)S(1)} %get-tuple-element.198), channel_id=1, source_target_pairs={{0,1},{1,0},{2,3},{3,2},{4,5},{5,4},{6,7},{7,6},{8,9},{9,8},{10,11... | collective-permute-start | bytes 2457608 | tf_op jit(solution)/shard_map/ppermute | solution.py:45
  41.1 12.3 %collective-permute-start.16 = (bf16[320,512]{1,0:T(8,128)(2,1)S(1)}, bf16[320,512]{1,0:T(8,128)(2,1)S(1)}, u32[]{:S(2)}, u32[]{:S(2)}) collective-permute-start(bf16[320,512]{1,0:T(8,128)(2,1)S(1)} %get-tuple-element.176.refs_8_), channel_id=1, source_target_pairs={{0,2},{1,3},{2,4},{3,5},{4,6},{5,7},{6,8},{7,9},{8,10},{9,11},{10,... | collective-permute-start | bytes 983048 | tf_op jit(solution)/shard_map/ppermute | solution.py:41
  41.2 12.2 %collective-permute-start.17 = (bf16[320,512]{1,0:T(8,128)(2,1)S(1)}, bf16[320,512]{1,0:T(8,128)(2,1)S(1)}, u32[]{:S(2)}, u32[]{:S(2)}) collective-permute-start(bf16[320,512]{1,0:T(8,128)(2,1)S(1)} %get-tuple-element.175.refs_7_), channel_id=1, source_target_pairs={{0,14},{1,15},{2,0},{3,1},{4,2},{5,3},{6,4},{7,5},{8,6},{9,7},{10,... | collective-permute-start | bytes 983048 | tf_op jit(solution)/shard_map/ppermute | solution.py:41
  47.2 13.3 %collective-permute-start.18 = (bf16[320,512]{1,0:T(8,128)(2,1)S(1)}, bf16[320,512]{1,0:T(8,128)(2,1)S(1)}, u32[]{:S(2)}, u32[]{:S(2)}) collective-permute-start(bf16[320,512]{1,0:T(8,128)(2,1)S(1)} %get-tuple-element.188.refs_5_), channel_id=1, source_target_pairs={{0,2},{1,3},{2,4},{3,5},{4,6},{5,7},{6,8},{7,9},{8,10},{9,11},{10,... | collective-permute-start | bytes 983048 | tf_op jit(solution)/shard_map/ppermute | solution.py:41
  47.3 13.2 %collective-permute-start.19 = (bf16[320,512]{1,0:T(8,128)(2,1)S(1)}, bf16[320,512]{1,0:T(8,128)(2,1)S(1)}, u32[]{:S(2)}, u32[]{:S(2)}) collective-permute-start(bf16[320,512]{1,0:T(8,128)(2,1)S(1)} %get-tuple-element.179.refs_2_), channel_id=1, source_target_pairs={{0,14},{1,15},{2,0},{3,1},{4,2},{5,3},{6,4},{7,5},{8,6},{9,7},{10,... | collective-permute-start | bytes 983048 | tf_op jit(solution)/shard_map/ppermute | solution.py:41
  53.7 14.5 %collective-permute-start.22 = (bf16[320,512]{1,0:T(8,128)(2,1)S(1)}, bf16[320,512]{1,0:T(8,128)(2,1)S(1)}, u32[]{:S(2)}, u32[]{:S(2)}) collective-permute-start(bf16[320,512]{1,0:T(8,128)(2,1)S(1)} %get-tuple-element.200), channel_id=1, source_target_pairs={{0,2},{1,3},{2,4},{3,5},{4,6},{5,7},{6,8},{7,9},{8,10},{9,11},{10,... | collective-permute-start | bytes 983048 | tf_op jit(solution)/shard_map/ppermute | solution.py:41
  53.8 14.4 %collective-permute-start.23 = (bf16[320,512]{1,0:T(8,128)(2,1)S(1)}, bf16[320,512]{1,0:T(8,128)(2,1)S(1)}, u32[]{:S(2)}, u32[]{:S(2)}) collective-permute-start(bf16[320,512]{1,0:T(8,128)(2,1)S(1)} %get-tuple-element.202), channel_id=1, source_target_pairs={{0,14},{1,15},{2,0},{3,1},{4,2},{5,3},{6,4},{7,5},{8,6},{9,7},{10,... | collective-permute-start | bytes 983048 | tf_op jit(solution)/shard_map/ppermute | solution.py:41
  60.7 13.8 %collective-permute-start.24 = (bf16[320,512]{1,0:T(8,128)(2,1)S(1)}, bf16[320,512]{1,0:T(8,128)(2,1)S(1)}, u32[]{:S(2)}, u32[]{:S(2)}) collective-permute-start(bf16[320,512]{1,0:T(8,128)(2,1)S(1)} %get-tuple-element.208), channel_id=1, source_target_pairs={{0,2},{1,3},{2,4},{3,5},{4,6},{5,7},{6,8},{7,9},{8,10},{9,11},{10,... | collective-permute-start | bytes 983048 | tf_op jit(solution)/shard_map/ppermute | solution.py:41
  60.9 24.6 %collective-permute-start.28 = (bf16[256,1280]{1,0:T(8,128)(2,1)S(1)}, bf16[256,1280]{1,0:T(8,128)(2,1)S(1)}, u32[]{:S(2)}, u32[]{:S(2)}) collective-permute-start(bf16[256,1280]{1,0:T(8,128)(2,1)S(1)} %get-tuple-element.216), channel_id=1, source_target_pairs={{0,1},{1,0},{2,3},{3,2},{4,5},{5,4},{6,7},{7,6},{8,9},{9,8},{10,11... | collective-permute-start | bytes 1966088 | tf_op jit(solution)/shard_map/ppermute | solution.py:45
  66.0 12.0 %collective-permute-start.25 = (bf16[320,512]{1,0:T(8,128)(2,1)S(1)}, bf16[320,512]{1,0:T(8,128)(2,1)S(1)}, u32[]{:S(2)}, u32[]{:S(2)}) collective-permute-start(bf16[320,512]{1,0:T(8,128)(2,1)S(1)} %get-tuple-element.210), channel_id=1, source_target_pairs={{0,14},{1,15},{2,0},{3,1},{4,2},{5,3},{6,4},{7,5},{8,6},{9,7},{10,... | collective-permute-start | bytes 983048 | tf_op jit(solution)/shard_map/ppermute | solution.py:41
  68.8 12.7 %collective-permute-start.29 = (bf16[320,512]{1,0:T(8,128)(2,1)S(1)}, bf16[320,512]{1,0:T(8,128)(2,1)S(1)}, u32[]{:S(2)}, u32[]{:S(2)}) collective-permute-start(bf16[320,512]{1,0:T(8,128)(2,1)S(1)} %get-tuple-element.218), channel_id=1, source_target_pairs={{0,2},{1,3},{2,4},{3,5},{4,6},{5,7},{6,8},{7,9},{8,10},{9,11},{10,... | collective-permute-start | bytes 983048 | tf_op jit(solution)/shard_map/ppermute | solution.py:41
  68.9 14.7 %collective-permute-start.30 = (bf16[320,512]{1,0:T(8,128)(2,1)S(1)}, bf16[320,512]{1,0:T(8,128)(2,1)S(1)}, u32[]{:S(2)}, u32[]{:S(2)}) collective-permute-start(bf16[320,512]{1,0:T(8,128)(2,1)S(1)} %get-tuple-element.220), channel_id=1, source_target_pairs={{0,14},{1,15},{2,0},{3,1},{4,2},{5,3},{6,4},{7,5},{8,6},{9,7},{10,... | collective-permute-start | bytes 983048 | tf_op jit(solution)/shard_map/ppermute | solution.py:41
  74.5 21.1 %collective-permute-start.20 = (bf16[256,1280]{1,0:T(8,128)(2,1)S(1)}, bf16[256,1280]{1,0:T(8,128)(2,1)S(1)}, u32[]{:S(2)}, u32[]{:S(2)}) collective-permute-start(bf16[256,1280]{1,0:T(8,128)(2,1)S(1)} %get-tuple-element.196), channel_id=1, source_target_pairs={{0,1},{1,0},{2,3},{3,2},{4,5},{5,4},{6,7},{7,6},{8,9},{9,8},{10,11... | collective-permute-start | bytes 1966088 | tf_op jit(solution)/shard_map/ppermute | solution.py:45
  78.2 11.5 %collective-permute-start.26 = (bf16[320,512]{1,0:T(8,128)(2,1)S(1)}, bf16[320,512]{1,0:T(8,128)(2,1)S(1)}, u32[]{:S(2)}, u32[]{:S(2)}) collective-permute-start(bf16[320,512]{1,0:T(8,128)(2,1)S(1)} %get-tuple-element.212), channel_id=1, source_target_pairs={{0,2},{1,3},{2,4},{3,5},{4,6},{5,7},{6,8},{7,9},{8,10},{9,11},{10,... | collective-permute-start | bytes 983048 | tf_op jit(solution)/shard_map/ppermute | solution.py:41
  81.5 10.6 %collective-permute-start.27 = (bf16[320,512]{1,0:T(8,128)(2,1)S(1)}, bf16[320,512]{1,0:T(8,128)(2,1)S(1)}, u32[]{:S(2)}, u32[]{:S(2)}) collective-permute-start(bf16[320,512]{1,0:T(8,128)(2,1)S(1)} %get-tuple-element.214), channel_id=1, source_target_pairs={{0,14},{1,15},{2,0},{3,1},{4,2},{5,3},{6,4},{7,5},{8,6},{9,7},{10,... | collective-permute-start | bytes 983048 | tf_op jit(solution)/shard_map/ppermute | solution.py:41
  83.9 14.2 %collective-permute-start.33 = (bf16[320,512]{1,0:T(8,128)(2,1)S(1)}, bf16[320,512]{1,0:T(8,128)(2,1)S(1)}, u32[]{:S(2)}, u32[]{:S(2)}) collective-permute-start(bf16[320,512]{1,0:T(8,128)(2,1)S(1)} %get-tuple-element.234), channel_id=1, source_target_pairs={{0,2},{1,3},{2,4},{3,5},{4,6},{5,7},{6,8},{7,9},{8,10},{9,11},{10,... | collective-permute-start | bytes 983048 | tf_op jit(solution)/shard_map/ppermute | solution.py:41
  85.4 13.8 %collective-permute-start.34 = (bf16[320,512]{1,0:T(8,128)(2,1)S(1)}, bf16[320,512]{1,0:T(8,128)(2,1)S(1)}, u32[]{:S(2)}, u32[]{:S(2)}) collective-permute-start(bf16[320,512]{1,0:T(8,128)(2,1)S(1)} %get-tuple-element.236), channel_id=1, source_target_pairs={{0,14},{1,15},{2,0},{3,1},{4,2},{5,3},{6,4},{7,5},{8,6},{9,7},{10,... | collective-permute-start | bytes 983048 | tf_op jit(solution)/shard_map/ppermute | solution.py:41
  92.4 13.7 %collective-permute-start.31 = (bf16[320,512]{1,0:T(8,128)(2,1)S(1)}, bf16[320,512]{1,0:T(8,128)(2,1)S(1)}, u32[]{:S(2)}, u32[]{:S(2)}) collective-permute-start(bf16[320,512]{1,0:T(8,128)(2,1)S(1)} %get-tuple-element.231), channel_id=1, source_target_pairs={{0,14},{1,15},{2,0},{3,1},{4,2},{5,3},{6,4},{7,5},{8,6},{9,7},{10,... | collective-permute-start | bytes 983048 | tf_op jit(solution)/shard_map/ppermute | solution.py:41
  95.6 10.6 %collective-permute-start.32 = (bf16[320,512]{1,0:T(8,128)(2,1)S(1)}, bf16[320,512]{1,0:T(8,128)(2,1)S(1)}, u32[]{:S(2)}, u32[]{:S(2)}) collective-permute-start(bf16[320,512]{1,0:T(8,128)(2,1)S(1)} %get-tuple-element.232), channel_id=1, source_target_pairs={{0,2},{1,3},{2,4},{3,5},{4,6},{5,7},{6,8},{7,9},{8,10},{9,11},{10,... | collective-permute-start | bytes 983048 | tf_op jit(solution)/shard_map/ppermute | solution.py:41
  110.6 15.6 %collective-permute-start.1 = (bf16[320,1024]{1,0:T(8,128)(2,1)S(1)}, bf16[320,1024]{1,0:T(8,128)(2,1)S(1)}, u32[]{:S(2)}, u32[]{:S(2)}) collective-permute-start(bf16[320,1024]{1,0:T(8,128)(2,1)S(1)} %get-tuple-element.54), channel_id=1, source_target_pairs={{0,32},{16,48},{32,64},{48,80},{64,96},{80,112},{96,128},{112,144}... | collective-permute-start | bytes 1966088 | tf_op jit(solution)/shard_map/cond/branch_1_fun/ppermute | solution.py:50
  (8 other events, 56.4 us)
